TPU v7x, 32 devices: a whole 2x2x4 slice. The times are simulated.
32 devices in a mesh: gy: 8 (over z, core), gz: 4 (over y, x).
Axes of the slice: x: 2, y: 2, z: 4, core: 2. Of those that a mesh axis runs over, the one named last changes fastest.
Arguments:
- volume: bfloat16 [4, 64, 32, 256], P(None, 'gy', 'gz'), may hold values from -6 to 6
- block_weight: bfloat16 [3, 3, 3, 256, 256], replicated, may hold values from -0.078125 to 0.078125
- aspp_weight: bfloat16 [3, 3, 3, 3, 256, 128], replicated, may hold values from -0.078125 to 0.078125
- proj_weight: bfloat16 [384, 128], replicated, may hold values from -0.3125 to 0.3125
- cotangent: bfloat16 [4, 64, 32, 128], P(None, 'gy', 'gz'), may hold values from -6 to 6
Outputs:
- pyramid_out: bfloat16 [4, 64, 32, 128], P(None, 'gy', 'gz')
- grad_volume: bfloat16 [4, 64, 32, 256], P(None, 'gy', 'gz')
- grad_block: float32 [1769472], P(('gy', 'gz'))
- grad_aspp: float32 [2654208], P(('gy', 'gz'))
- grad_proj: float32 [49152], P(('gy', 'gz'))
All inputs are finite; a program needn't handle non-finite values.
Results may differ from a plain program's by a relative error of at most 0.01.
Values may be sent and summed in bfloat16 or wider, within the bound.
A program may use at most 192 MiB of HBM per device.

v0:
```python
import jax
import jax.numpy as jnp
from jax import lax
from jax.sharding import PartitionSpec as P

dilation_rates = (2, 4, 8)


def extended(cells, sides, width):
    for axis, dim in sides:
        count = lax.axis_size(axis)
        ends = count - 1
        head = lax.slice_in_dim(cells, 0, width, axis=dim)
        tail = lax.slice_in_dim(cells, cells.shape[dim] - width, cells.shape[dim], axis=dim)
        cells = jnp.concatenate(
            [
                lax.ppermute(tail, axis, [(i, (i + 1) % count) for i in range(ends)]),
                cells,
                lax.ppermute(head, axis, [((i + 1) % count, i) for i in range(ends)]),
            ],
            axis=dim,
        )
    return cells


def silu_slope(value):
    sigma = jax.nn.sigmoid(value)
    return sigma * (1.0 + value * (1.0 - sigma))


def tap_conv(padded, kernel, dilation):
    depth = padded.shape[0] - 2 * dilation
    rows = padded.shape[1] - 2 * dilation
    cols = padded.shape[2] - 2 * dilation
    in_width = padded.shape[3]
    out_width = kernel.shape[-1]
    total = jnp.zeros((depth * rows * cols, out_width), jnp.float32)
    for first in range(3):
        for second in range(3):
            for third in range(3):
                piece = padded[
                    first * dilation : first * dilation + depth,
                    second * dilation : second * dilation + rows,
                    third * dilation : third * dilation + cols,
                ]
                total = total + jnp.dot(
                    piece.reshape(-1, in_width),
                    kernel[first, second, third],
                    preferred_element_type=jnp.float32,
                )
    return total.reshape(depth, rows, cols, out_width)


def weight_grad(padded, grad_out, dilation):
    depth, rows, cols, out_width = grad_out.shape
    in_width = padded.shape[3]
    grad_rows = grad_out.reshape(-1, out_width)
    taps = []
    for first in range(3):
        for second in range(3):
            for third in range(3):
                piece = padded[
                    first * dilation : first * dilation + depth,
                    second * dilation : second * dilation + rows,
                    third * dilation : third * dilation + cols,
                ]
                taps.append(
                    jnp.dot(
                        piece.reshape(-1, in_width).T, grad_rows, preferred_element_type=jnp.float32
                    )
                )
    return jnp.stack(taps).reshape(3, 3, 3, in_width, out_width)


def flipped(kernel):
    return jnp.swapaxes(kernel[::-1, ::-1, ::-1], 3, 4)


def deepen(source, dilation):
    return jnp.pad(source, ((dilation, dilation), (0, 0), (0, 0), (0, 0)))


def local(volume, block_weight, aspp_weight, proj_weight, cotangent):
    layer_count, row_count, col_count, channels = volume.shape
    branch_width = aspp_weight.shape[-1]
    widest_rate = max(dilation_rates)
    volume_rim = extended(volume, (("gy", 1), ("gz", 2)), 1)
    volume_padded = deepen(volume_rim, 1)
    pre_block = tap_conv(volume_padded, block_weight, 1)
    hidden = jax.nn.silu(pre_block).astype(jnp.bfloat16)
    padded_list = []
    for dilation in dilation_rates:
        padded_list.append(deepen(extended(hidden, (("gy", 1), ("gz", 2)), dilation), dilation))
    branch_list = []
    for branch, dilation in enumerate(dilation_rates):
        branch_list.append(tap_conv(padded_list[branch], aspp_weight[branch], dilation))
    branch_pre = jnp.concatenate(branch_list, -1).reshape(-1, 3 * branch_width)
    joined_rows = jax.nn.silu(branch_pre).astype(jnp.bfloat16)
    pyramid_out = (
        jnp.dot(joined_rows, proj_weight, preferred_element_type=jnp.float32)
        .reshape(layer_count, row_count, col_count, branch_width)
        .astype(jnp.bfloat16)
    )
    grad_rows = cotangent.reshape(-1, branch_width)
    grad_proj = jnp.dot(joined_rows.T, grad_rows, preferred_element_type=jnp.float32)
    proj_back = jnp.dot(grad_rows, proj_weight.T, preferred_element_type=jnp.float32)
    grad_joined = (
        (proj_back * silu_slope(branch_pre))
        .astype(jnp.bfloat16)
        .reshape(layer_count, row_count, col_count, 3 * branch_width)
    )
    aspp_list = []
    for branch, dilation in enumerate(dilation_rates):
        grad_piece = grad_joined[..., branch * branch_width : (branch + 1) * branch_width]
        aspp_list.append(weight_grad(padded_list[branch], grad_piece, dilation))
    grad_aspp = jnp.stack(aspp_list).reshape(-1)
    grad_wide = extended(grad_joined, (("gy", 1), ("gz", 2)), widest_rate)
    grad_hidden = jnp.zeros((layer_count, row_count, col_count, channels), jnp.float32)
    for branch, dilation in enumerate(dilation_rates):
        start = widest_rate - dilation
        grad_piece = grad_wide[
            :,
            start : start + row_count + 2 * dilation,
            start : start + col_count + 2 * dilation,
            branch * branch_width : (branch + 1) * branch_width,
        ]
        grad_hidden = grad_hidden + tap_conv(
            deepen(grad_piece, dilation), flipped(aspp_weight[branch]), dilation
        )
    grad_pre = (grad_hidden * silu_slope(pre_block)).astype(jnp.bfloat16)
    grad_pre_rim = extended(grad_pre, (("gy", 1), ("gz", 2)), 1)
    grad_volume = tap_conv(deepen(grad_pre_rim, 1), flipped(block_weight), 1)
    grad_volume = grad_volume.astype(jnp.bfloat16)
    grad_block = weight_grad(volume_padded, grad_pre, 1).reshape(-1)
    block_share, aspp_share, proj_share = (
        lax.psum_scatter(grad_block, ("gy", "gz"), scatter_dimension=0, tiled=True),
        lax.psum_scatter(grad_aspp, ("gy", "gz"), scatter_dimension=0, tiled=True),
        lax.psum_scatter(grad_proj.reshape(-1), ("gy", "gz"), scatter_dimension=0, tiled=True),
    )
    return (pyramid_out, grad_volume, block_share, aspp_share, proj_share)


def solution(mesh):
    in_specs = (P(None, "gy", "gz", None), P(), P(), P(), P(None, "gy", "gz", None))
    out_specs = (
        P(None, "gy", "gz", None),
        P(None, "gy", "gz", None),
        P(("gy", "gz")),
        P(("gy", "gz")),
        P(("gy", "gz")),
    )
    return jax.shard_map(local, mesh=mesh, in_specs=in_specs, out_specs=out_specs, check_vma=False)
```

profile of v0, /device:TPU:0, one launch (start us, length us, event | category | flops | bytes accessed | tf_op | source)
XLA Modules:
  0.0 493.5 jit_solution(6248469265983734403)
XLA Ops:
  8.0 2.3 collective-permute-start
  10.3 1.3 collective-permute-start.1
  11.6 2.9 slice_bitcast_fusion.2
  22.5 1.4 collective-permute-start.3
  23.9 4.9 collective-permute-start.2
  29.0 1.4 collective-permute-done.2
  37.0 1.3 collective-permute-start.13
  38.3 4.4 collective-permute-start.12
  43.1 1.3 collective-permute-start.5
  44.4 5.4 %collective-permute-start.4 = (bf16[4,2,8,256]{3,2,1,0:T(8,128)(2,1)S(1)}, bf16[4,2,8,256]{3,2,1,0:T(8,128)(2,1)S(1)}, u32[]{:S(2)}, u32[]{:S(2)}) collective-permute-start(bf16[4,2,8,256]{3,2,1,0:T(8,128)(2,1)S(1)} %get-tuple-element.173), channel_id=1, source_target_pairs={{0,4},{4,8},{8,12},{12,16},{16,20},{20,24},{24,28},{1,5},{5,9},{9,... | collective-permute-start | bytes 98312 | tf_op jit(solution)/shard_map/ppermute | solution.py:17
  49.9 1.3 collective-permute-start.9
  51.2 4.3 collective-permute-start.8
  55.5 4.3 collective-permute-start.6
  59.8 1.3 collective-permute-start.7
  61.3 1.3 collective-permute-start.11
  62.6 6.4 %collective-permute-start.10 = (bf16[4,16,4,256]{3,2,1,0:T(4,128)(2,1)S(1)}, bf16[4,16,4,256]{3,2,1,0:T(4,128)(2,1)S(1)}, u32[]{:S(2)}, u32[]{:S(2)}) collective-permute-start(bf16[4,16,4,256]{3,2,1,0:T(4,128)(2,1)S(1)} %get-tuple-element.136), channel_id=1, source_target_pairs={{0,1},{1,2},{2,3},{4,5},{5,6},{6,7},{8,9},{9,10},{10,11},{12,13},{... | collective-permute-start | bytes 393224 | tf_op jit(solution)/shard_map/ppermute | solution.py:17
  72.3 1.3 collective-permute-start.15
  73.6 5.7 %collective-permute-start.14 = (bf16[4,24,8,256]{3,2,1,0:T(8,128)(2,1)S(1)}, bf16[4,24,8,256]{3,2,1,0:T(8,128)(2,1)S(1)}, u32[]{:S(2)}, u32[]{:S(2)}) collective-permute-start(bf16[4,24,8,256]{3,2,1,0:T(8,128)(2,1)S(1)} %pad_maximum_fusion.3), channel_id=1, source_target_pairs={{0,1},{1,2},{2,3},{4,5},{5,6},{6,7},{8,9},{9,10},{10,11},{12,13},{... | collective-permute-start | bytes 1179656 | tf_op jit(solution)/shard_map/ppermute | solution.py:17
  85.5 1.3 collective-permute-done.15
  87.1 1.4 collective-permute-done.14
  91.1 1.3 collective-permute-start.17
  92.4 3.0 collective-permute-start.16
  101.8 1.3 convolution_bitcast_fusion
  104.0 1.3 collective-permute-start.19
  105.3 9.2 %collective-permute-start.18 = (bf16[4,24,8,384]{3,2,1,0:T(8,128)(2,1)}, bf16[4,24,8,384]{3,2,1,0:T(8,128)(2,1)S(1)}, u32[]{:S(2)}, u32[]{:S(2)}) collective-permute-start(bf16[4,24,8,384]{3,2,1,0:T(8,128)(2,1)} %pad_maximum_fusion.1), channel_id=1, source_target_pairs={{0,1},{1,2},{2,3},{4,5},{5,6},{6,7},{8,9},{9,10},{10,11},{12,13},{... | collective-permute-start | bytes 1769480 | tf_op jit(solution)/shard_map/ppermute | solution.py:17
  122.7 8.2 %pad_maximum_fusion = f32[3,3,3,3,256,128]{5,4,3,2,1,0:T(8,128)} fusion(f32[1,3,3,3,256,128]{5,4,3,2,1,0:T(8,128)} %bitcast.1662, f32[1,3,3,3,256,128]{5,4,3,2,1,0:T(8,128)S(1)} %bitcast.1661, f32[1,3,3,3,256,128]{5,4,3,2,1,0:T(8,128)} %bitcast.1663), kind=kLoop, calls=%fused_computation | loop fusion | flops 5308416 | bytes 21233664 | tf_op jit(solution)/shard_map/stack | solution.py:116
  144.1 0.9 fusion.51
  145.0 0.9 fusion.50
  146.0 1.0 fusion.49
  151.6 0.9 fusion.28
  152.5 0.9 fusion.43
  153.5 1.0 fusion.42
  158.2 0.9 fusion.38
  162.8 1.0 fusion.33
  163.8 1.0 fusion.32
  166.6 1.0 fusion.29
  167.6 9.8 %copy.86 = f32[864,2,8,128]{3,1,2,0:T(2,128)} copy(f32[864,2,8,128]{3,2,1,0:T(8,128)} %bitcast.741) | data formatting | bytes 14155776
  177.4 2.4 reverse_bitcast_fusion
  179.8 1.3 collective-permute-start.21
  181.1 3.8 collective-permute-start.20
  185.9 8.8 %collective-permute-start.22 = (bf16[4,10,1,256]{3,2,1,0:T(2,128)(2,1)S(1)}, bf16[4,10,1,256]{3,2,1,0:T(2,128)(2,1)S(1)}, u32[]{:S(2)}, u32[]{:S(2)}) collective-permute-start(bf16[4,10,1,256]{3,2,1,0:T(2,128)(2,1)S(1)} %get-tuple-element.160), channel_id=1, source_target_pairs={{0,1},{1,2},{2,3},{4,5},{5,6},{6,7},{8,9},{9,10},{10,11},{12,13},{... | collective-permute-start | bytes 61448 | tf_op jit(solution)/shard_map/ppermute | solution.py:17
  194.7 1.3 collective-permute-start.23
  196.1 1.2 collective-permute-done.22
  197.3 5.9 %collective-permute-done.23 = bf16[4,10,1,256]{3,2,1,0:T(2,128)(2,1)S(1)} collective-permute-done((bf16[4,10,1,256]{3,2,1,0:T(2,128)(2,1)S(1)}, bf16[4,10,1,256]{3,2,1,0:T(2,128)(2,1)S(1)}, u32[]{:S(2)}, u32[]{:S(2)}) %collective-permute-start.23) | collective-permute-done | bytes 20512 | tf_op jit(solution)/shard_map/ppermute | solution.py:19
  210.9 271.1 %all-reduce.10.cloned.1.call-done = (f32[1769472]{0:T(1024)}, f32[2654208]{0:T(1024)}, f32[49152]{0:T(1024)}) async-done(((f32[1769472]{0:T(1024)}, f32[2654208]{0:T(1024)}, f32[49152]{0:T(1024)}), (f32[1769472]{0:T(1024)}, f32[2654208]{0:T(1024)}, f32[49152]{0:T(1024)})) %all-reduce.10.cloned.1.call-update) | async-done | bytes 17891344
  481.9 1.6 dynamic-slice
  483.6 1.7 dynamic-slice.1
  485.3 1.4 dynamic-slice.2
  (436 shorter events, 77.5 us)
Async XLA Ops:
  7.2 83.7 %copy-start = (bf16[384,128]{1,0:T(8,128)(2,1)S(1)}, bf16[384,128]{1,0:T(8,128)(2,1)}, u32[]{:S(2)}) copy-start(bf16[384,128]{1,0:T(8,128)(2,1)} %param.8) | copy-start | bytes 294916
  7.2 474.8 %all-reduce.10.cloned.1.call-start = ((), (), s32[]{:S(2)}) async-start(), calls=%async_computation | async-start | bytes 35782656
  8.0 14.3 %collective-permute-start = (bf16[4,1,8,256]{3,2,1,0:T(8,128)(2,1)S(1)}, bf16[4,1,8,256]{3,2,1,0:T(8,128)(2,1)S(1)}, u32[]{:S(2)}, u32[]{:S(2)}) collective-permute-start(bf16[4,1,8,256]{3,2,1,0:T(8,128)(2,1)S(1)} %get-tuple-element.181), channel_id=1, source_target_pairs={{0,4},{4,8},{8,12},{12,16},{16,20},{20,24},{24,28},{1,5},{5,9},{9,... | collective-permute-start | bytes 49160 | tf_op jit(solution)/shard_map/ppermute | solution.py:17
  10.3 12.1 %collective-permute-start.1 = (bf16[4,1,8,256]{3,2,1,0:T(8,128)(2,1)S(1)}, bf16[4,1,8,256]{3,2,1,0:T(8,128)(2,1)S(1)}, u32[]{:S(2)}, u32[]{:S(2)}) collective-permute-start(bf16[4,1,8,256]{3,2,1,0:T(8,128)(2,1)S(1)} %get-tuple-element.180), channel_id=1, source_target_pairs={{4,0},{8,4},{12,8},{16,12},{20,16},{24,20},{28,24},{5,1},{9,5},{13... | collective-permute-start | bytes 49160 | tf_op jit(solution)/shard_map/ppermute | solution.py:19
  21.4 7.4 %copy-start.1 = (bf16[3,3,3,256,256]{4,3,2,1,0:T(8,128)(2,1)S(1)}, bf16[3,3,3,256,256]{4,3,2,1,0:T(8,128)(2,1)}, u32[]{:S(2)}) copy-start(bf16[3,3,3,256,256]{4,3,2,1,0:T(8,128)(2,1)} %param.6) | copy-start | bytes 10616836
  22.4 6.7 %copy-start.19 = (bf16[4,9,8,256]{3,2,1,0:T(8,128)(2,1)}, bf16[4,9,8,256]{3,2,1,0:T(8,128)(2,1)S(1)}, u32[]{:S(2)}) copy-start(bf16[4,9,8,256]{3,2,1,0:T(8,128)(2,1)S(1)} %get-tuple-element.177) | copy-start | bytes 442372
  22.4 6.6 %copy-start.17 = (bf16[4,9,8,256]{3,2,1,0:T(8,128)(2,1)}, bf16[4,9,8,256]{3,2,1,0:T(8,128)(2,1)S(1)}, u32[]{:S(2)}) copy-start(bf16[4,9,8,256]{3,2,1,0:T(8,128)(2,1)S(1)} %get-tuple-element.184) | copy-start | bytes 442372
  22.5 6.5 %collective-permute-start.3 = (bf16[4,10,1,256]{3,2,1,0:T(2,128)(2,1)S(1)}, bf16[4,10,1,256]{3,2,1,0:T(2,128)(2,1)S(1)}, u32[]{:S(2)}, u32[]{:S(2)}) collective-permute-start(bf16[4,10,1,256]{3,2,1,0:T(2,128)(2,1)S(1)} %get-tuple-element.166), channel_id=1, source_target_pairs={{1,0},{2,1},{3,2},{5,4},{6,5},{7,6},{9,8},{10,9},{11,10},{13,12},{... | collective-permute-start | bytes 61448 | tf_op jit(solution)/shard_map/ppermute | solution.py:19
  23.9 6.5 %collective-permute-start.2 = (bf16[4,10,1,256]{3,2,1,0:T(2,128)(2,1)S(1)}, bf16[4,10,1,256]{3,2,1,0:T(2,128)(2,1)S(1)}, u32[]{:S(2)}, u32[]{:S(2)}) collective-permute-start(bf16[4,10,1,256]{3,2,1,0:T(2,128)(2,1)S(1)} %get-tuple-element.165), channel_id=1, source_target_pairs={{0,1},{1,2},{2,3},{4,5},{5,6},{6,7},{8,9},{9,10},{10,11},{12,13},{... | collective-permute-start | bytes 61448 | tf_op jit(solution)/shard_map/ppermute | solution.py:17
  31.5 2.4 copy-start.15
  31.5 2.8 copy-start.13
  31.5 3.0 copy-start.11
  31.5 3.4 copy-start.9
  37.0 35.2 %collective-permute-start.13 = (bf16[4,8,8,256]{3,2,1,0:T(8,128)(2,1)S(1)}, bf16[4,8,8,256]{3,2,1,0:T(8,128)(2,1)S(1)}, u32[]{:S(2)}, u32[]{:S(2)}) collective-permute-start(bf16[4,8,8,256]{3,2,1,0:T(8,128)(2,1)S(1)} %multiply_convert_fusion.5), channel_id=1, source_target_pairs={{4,0},{8,4},{12,8},{16,12},{20,16},{24,20},{28,24},{5,1},{9,5},{13... | collective-permute-start | bytes 393224 | tf_op jit(solution)/shard_map/ppermute | solution.py:19
  38.3 33.9 %collective-permute-start.12 = (bf16[4,8,8,256]{3,2,1,0:T(8,128)(2,1)S(1)}, bf16[4,8,8,256]{3,2,1,0:T(8,128)(2,1)S(1)}, u32[]{:S(2)}, u32[]{:S(2)}) collective-permute-start(bf16[4,8,8,256]{3,2,1,0:T(8,128)(2,1)S(1)} %multiply_convert_fusion.5), channel_id=1, source_target_pairs={{0,4},{4,8},{8,12},{12,16},{16,20},{20,24},{24,28},{1,5},{5,9},{9,... | collective-permute-start | bytes 393224 | tf_op jit(solution)/shard_map/ppermute | solution.py:17
  43.1 8.0 %collective-permute-start.5 = (bf16[4,2,8,256]{3,2,1,0:T(8,128)(2,1)S(1)}, bf16[4,2,8,256]{3,2,1,0:T(8,128)(2,1)S(1)}, u32[]{:S(2)}, u32[]{:S(2)}) collective-permute-start(bf16[4,2,8,256]{3,2,1,0:T(8,128)(2,1)S(1)} %get-tuple-element.174), channel_id=1, source_target_pairs={{4,0},{8,4},{12,8},{16,12},{20,16},{24,20},{28,24},{5,1},{9,5},{13... | collective-permute-start | bytes 98312 | tf_op jit(solution)/shard_map/ppermute | solution.py:19
  44.4 11.0 %collective-permute-start.4 = (bf16[4,2,8,256]{3,2,1,0:T(8,128)(2,1)S(1)}, bf16[4,2,8,256]{3,2,1,0:T(8,128)(2,1)S(1)}, u32[]{:S(2)}, u32[]{:S(2)}) collective-permute-start(bf16[4,2,8,256]{3,2,1,0:T(8,128)(2,1)S(1)} %get-tuple-element.173), channel_id=1, source_target_pairs={{0,4},{4,8},{8,12},{12,16},{16,20},{20,24},{24,28},{1,5},{5,9},{9,... | collective-permute-start | bytes 98312 | tf_op jit(solution)/shard_map/ppermute | solution.py:17
  49.9 10.0 %collective-permute-start.9 = (bf16[4,4,8,256]{3,2,1,0:T(8,128)(2,1)S(1)}, bf16[4,4,8,256]{3,2,1,0:T(8,128)(2,1)S(1)}, u32[]{:S(2)}, u32[]{:S(2)}) collective-permute-start(bf16[4,4,8,256]{3,2,1,0:T(8,128)(2,1)S(1)} %get-tuple-element.176), channel_id=1, source_target_pairs={{4,0},{8,4},{12,8},{16,12},{20,16},{24,20},{28,24},{5,1},{9,5},{13... | collective-permute-start | bytes 196616 | tf_op jit(solution)/shard_map/ppermute | solution.py:19
  51.2 10.0 %collective-permute-start.8 = (bf16[4,4,8,256]{3,2,1,0:T(8,128)(2,1)S(1)}, bf16[4,4,8,256]{3,2,1,0:T(8,128)(2,1)S(1)}, u32[]{:S(2)}, u32[]{:S(2)}) collective-permute-start(bf16[4,4,8,256]{3,2,1,0:T(8,128)(2,1)S(1)} %get-tuple-element.175), channel_id=1, source_target_pairs={{0,4},{4,8},{8,12},{12,16},{16,20},{20,24},{24,28},{1,5},{5,9},{9,... | collective-permute-start | bytes 196616 | tf_op jit(solution)/shard_map/ppermute | solution.py:17
  55.5 7.0 %collective-permute-start.6 = (bf16[4,12,2,256]{3,2,1,0:T(2,128)(2,1)S(1)}, bf16[4,12,2,256]{3,2,1,0:T(2,128)(2,1)S(1)}, u32[]{:S(2)}, u32[]{:S(2)}) collective-permute-start(bf16[4,12,2,256]{3,2,1,0:T(2,128)(2,1)S(1)} %get-tuple-element.154), channel_id=1, source_target_pairs={{0,1},{1,2},{2,3},{4,5},{5,6},{6,7},{8,9},{9,10},{10,11},{12,13},{... | collective-permute-start | bytes 147464 | tf_op jit(solution)/shard_map/ppermute | solution.py:17
  59.8 9.2 %collective-permute-start.7 = (bf16[4,12,2,256]{3,2,1,0:T(2,128)(2,1)S(1)}, bf16[4,12,2,256]{3,2,1,0:T(2,128)(2,1)S(1)}, u32[]{:S(2)}, u32[]{:S(2)}) collective-permute-start(bf16[4,12,2,256]{3,2,1,0:T(2,128)(2,1)S(1)} %get-tuple-element.155), channel_id=1, source_target_pairs={{1,0},{2,1},{3,2},{5,4},{6,5},{7,6},{9,8},{10,9},{11,10},{13,12},{... | collective-permute-start | bytes 147464 | tf_op jit(solution)/shard_map/ppermute | solution.py:19
  61.3 18.3 %collective-permute-start.11 = (bf16[4,16,4,256]{3,2,1,0:T(4,128)(2,1)S(1)}, bf16[4,16,4,256]{3,2,1,0:T(4,128)(2,1)S(1)}, u32[]{:S(2)}, u32[]{:S(2)}) collective-permute-start(bf16[4,16,4,256]{3,2,1,0:T(4,128)(2,1)S(1)} %get-tuple-element.137), channel_id=1, source_target_pairs={{1,0},{2,1},{3,2},{5,4},{6,5},{7,6},{9,8},{10,9},{11,10},{13,12},{... | collective-permute-start | bytes 393224 | tf_op jit(solution)/shard_map/ppermute | solution.py:19
  62.6 17.6 %collective-permute-start.10 = (bf16[4,16,4,256]{3,2,1,0:T(4,128)(2,1)S(1)}, bf16[4,16,4,256]{3,2,1,0:T(4,128)(2,1)S(1)}, u32[]{:S(2)}, u32[]{:S(2)}) collective-permute-start(bf16[4,16,4,256]{3,2,1,0:T(4,128)(2,1)S(1)} %get-tuple-element.136), channel_id=1, source_target_pairs={{0,1},{1,2},{2,3},{4,5},{5,6},{6,7},{8,9},{9,10},{10,11},{12,13},{... | collective-permute-start | bytes 393224 | tf_op jit(solution)/shard_map/ppermute | solution.py:17
  72.3 14.6 %collective-permute-start.15 = (bf16[4,24,8,256]{3,2,1,0:T(8,128)(2,1)S(1)}, bf16[4,24,8,256]{3,2,1,0:T(8,128)(2,1)S(1)}, u32[]{:S(2)}, u32[]{:S(2)}) collective-permute-start(bf16[4,24,8,256]{3,2,1,0:T(8,128)(2,1)S(1)} %pad_maximum_fusion.3), channel_id=1, source_target_pairs={{1,0},{2,1},{3,2},{5,4},{6,5},{7,6},{9,8},{10,9},{11,10},{13,12},{... | collective-permute-start | bytes 1179656 | tf_op jit(solution)/shard_map/ppermute | solution.py:19
  73.6 14.9 %collective-permute-start.14 = (bf16[4,24,8,256]{3,2,1,0:T(8,128)(2,1)S(1)}, bf16[4,24,8,256]{3,2,1,0:T(8,128)(2,1)S(1)}, u32[]{:S(2)}, u32[]{:S(2)}) collective-permute-start(bf16[4,24,8,256]{3,2,1,0:T(8,128)(2,1)S(1)} %pad_maximum_fusion.3), channel_id=1, source_target_pairs={{0,1},{1,2},{2,3},{4,5},{5,6},{6,7},{8,9},{9,10},{10,11},{12,13},{... | collective-permute-start | bytes 1179656 | tf_op jit(solution)/shard_map/ppermute | solution.py:17
  85.3 16.4 %copy-start.23 = (f32[256,128]{1,0:T(8,128)}, f32[256,128]{1,0:T(8,128)S(1)}, u32[]{:S(2)}) copy-start(f32[256,128]{1,0:T(8,128)S(1)} %convolution_add_fusion.119) | copy-start | bytes 393220
  85.5 16.2 %copy-start.21 = (f32[256,128]{1,0:T(8,128)}, f32[256,128]{1,0:T(8,128)S(1)}, u32[]{:S(2)}) copy-start(f32[256,128]{1,0:T(8,128)S(1)} %convolution_add_fusion.137) | copy-start | bytes 393220
  86.9 3.9 copy-start.27
  90.8 11.0 %copy-start.25 = (f32[256,128]{1,0:T(8,128)}, f32[256,128]{1,0:T(8,128)S(1)}, u32[]{:S(2)}) copy-start(f32[256,128]{1,0:T(8,128)S(1)} %convolution_add_fusion.101) | copy-start | bytes 393220
  91.1 12.0 %collective-permute-start.17 = (bf16[4,8,8,384]{3,2,1,0:T(8,128)(2,1)S(1)}, bf16[4,8,8,384]{3,2,1,0:T(8,128)(2,1)S(1)}, u32[]{:S(2)}, u32[]{:S(2)}) collective-permute-start(bf16[4,8,8,384]{3,2,1,0:T(8,128)(2,1)S(1)} %bitcast.1608), channel_id=1, source_target_pairs={{4,0},{8,4},{12,8},{16,12},{20,16},{24,20},{28,24},{5,1},{9,5},{13... | collective-permute-start | bytes 589832 | tf_op jit(solution)/shard_map/ppermute | solution.py:19
  92.4 10.7 %collective-permute-start.16 = (bf16[4,8,8,384]{3,2,1,0:T(8,128)(2,1)S(1)}, bf16[4,8,8,384]{3,2,1,0:T(8,128)(2,1)S(1)}, u32[]{:S(2)}, u32[]{:S(2)}) collective-permute-start(bf16[4,8,8,384]{3,2,1,0:T(8,128)(2,1)S(1)} %bitcast.1609), channel_id=1, source_target_pairs={{0,4},{4,8},{8,12},{12,16},{16,20},{20,24},{24,28},{1,5},{5,9},{9,... | collective-permute-start | bytes 589832 | tf_op jit(solution)/shard_map/ppermute | solution.py:17
  101.8 16.7 %copy-start.3 = (f32[27,256,128]{2,1,0:T(8,128)}, f32[27,256,128]{2,1,0:T(8,128)S(1)}, u32[]{:S(2)}) copy-start(f32[27,256,128]{2,1,0:T(8,128)S(1)} %fusion.81) | copy-start | bytes 10616836
  104.0 26.9 %collective-permute-start.19 = (bf16[4,24,8,384]{3,2,1,0:T(8,128)(2,1)}, bf16[4,24,8,384]{3,2,1,0:T(8,128)(2,1)S(1)}, u32[]{:S(2)}, u32[]{:S(2)}) collective-permute-start(bf16[4,24,8,384]{3,2,1,0:T(8,128)(2,1)} %pad_maximum_fusion.1), channel_id=1, source_target_pairs={{1,0},{2,1},{3,2},{5,4},{6,5},{7,6},{9,8},{10,9},{11,10},{13,12},{... | collective-permute-start | bytes 1769480 | tf_op jit(solution)/shard_map/ppermute | solution.py:19
  105.3 25.6 %collective-permute-start.18 = (bf16[4,24,8,384]{3,2,1,0:T(8,128)(2,1)}, bf16[4,24,8,384]{3,2,1,0:T(8,128)(2,1)S(1)}, u32[]{:S(2)}, u32[]{:S(2)}) collective-permute-start(bf16[4,24,8,384]{3,2,1,0:T(8,128)(2,1)} %pad_maximum_fusion.1), channel_id=1, source_target_pairs={{0,1},{1,2},{2,3},{4,5},{5,6},{6,7},{8,9},{9,10},{10,11},{12,13},{... | collective-permute-start | bytes 1769480 | tf_op jit(solution)/shard_map/ppermute | solution.py:17
  119.4 2.4 copy-start.2
  134.0 2.3 copy-start.6
  149.7 1.9 copy-start.20
  150.7 1.9 copy-start.14
  151.6 1.9 copy-start.12
  152.5 2.8 copy-start.10
  155.4 1.9 copy-start.18
  177.4 7.6 %copy-start.22 = (f32[256,128]{1,0:T(8,128)S(1)}, f32[256,128]{1,0:T(8,128)}, u32[]{:S(2)}) copy-start(f32[256,128]{1,0:T(8,128)} %copy-done.21) | copy-start | bytes 393220
  177.4 7.6 %copy-start.24 = (f32[256,128]{1,0:T(8,128)S(1)}, f32[256,128]{1,0:T(8,128)}, u32[]{:S(2)}) copy-start(f32[256,128]{1,0:T(8,128)} %copy-done.23) | copy-start | bytes 393220
  177.4 7.6 %copy-start.26 = (f32[256,128]{1,0:T(8,128)S(1)}, f32[256,128]{1,0:T(8,128)}, u32[]{:S(2)}) copy-start(f32[256,128]{1,0:T(8,128)} %copy-done.25) | copy-start | bytes 393220
  179.8 6.0 %collective-permute-start.21 = (bf16[4,1,8,256]{3,2,1,0:T(8,128)(2,1)S(1)}, bf16[4,1,8,256]{3,2,1,0:T(8,128)(2,1)S(1)}, u32[]{:S(2)}, u32[]{:S(2)}) collective-permute-start(bf16[4,1,8,256]{3,2,1,0:T(8,128)(2,1)S(1)} %get-tuple-element.170), channel_id=1, source_target_pairs={{4,0},{8,4},{12,8},{16,12},{20,16},{24,20},{28,24},{5,1},{9,5},{13... | collective-permute-start | bytes 49160 | tf_op jit(solution)/shard_map/ppermute | solution.py:19
  181.1 4.7 collective-permute-start.20
  185.9 11.4 %collective-permute-start.22 = (bf16[4,10,1,256]{3,2,1,0:T(2,128)(2,1)S(1)}, bf16[4,10,1,256]{3,2,1,0:T(2,128)(2,1)S(1)}, u32[]{:S(2)}, u32[]{:S(2)}) collective-permute-start(bf16[4,10,1,256]{3,2,1,0:T(2,128)(2,1)S(1)} %get-tuple-element.160), channel_id=1, source_target_pairs={{0,1},{1,2},{2,3},{4,5},{5,6},{6,7},{8,9},{9,10},{10,11},{12,13},{... | collective-permute-start | bytes 61448 | tf_op jit(solution)/shard_map/ppermute | solution.py:17
  194.7 8.5 %collective-permute-start.23 = (bf16[4,10,1,256]{3,2,1,0:T(2,128)(2,1)S(1)}, bf16[4,10,1,256]{3,2,1,0:T(2,128)(2,1)S(1)}, u32[]{:S(2)}, u32[]{:S(2)}) collective-permute-start(bf16[4,10,1,256]{3,2,1,0:T(2,128)(2,1)S(1)} %get-tuple-element.161), channel_id=1, source_target_pairs={{1,0},{2,1},{3,2},{5,4},{6,5},{7,6},{9,8},{10,9},{11,10},{13,12},{... | collective-permute-start | bytes 61448 | tf_op jit(solution)/shard_map/ppermute | solution.py:19
  (5 other events, 7.4 us)
Sparse Core Ops, SparseCore 0:
  177.5 304.4 all-reduce.9
where the time goes:
time: 494 us
  waiting for transfers between devices  282 us (57%)
  matrix products  80.6 us (16%)
  starting transfers between devices  78.1 us (16%)
  local copies, waits for them, and re-layouts  23.7 us (5%)
  between operations  16.9 us (3%)
  other arithmetic  11.9 us (2%)
    unnamed x2, waiting for transfers between devices  271 us
    ppermute x12, starting transfers between devices, extended(): lax.ppermute(tail, axis, [(i, (i + 1) % count) for i in range(ends)])  62.5 us
    dot_general x216, matrix products, tap_conv(): jnp.dot(piece.reshape(-1, in_width), kernel[first, second, third], prefer...  42.1 us
    dot_general x74, matrix products, weight_grad(): jnp.dot(piece.reshape(-1, in_width).T, grad_rows, preferred_element_type=...  36.1 us
    ppermute x12, starting transfers between devices, extended(): lax.ppermute(head, axis, [((i + 1) % count, i) for i in range(ends)])  15.6 us
    unnamed x93, local copies, waits for them, and re-layouts  15.4 us
  transfers between devices with their start and end apart: 25, of which 6 were waited for; matrix products, arithmetic and copies ran while one was open for 11% of the time, Pallas kernels for 0%

commit v1 on v0

v1 whole, which is shorter than its diff:
```python
import math

import jax
import jax.numpy as jnp
import numpy as np
from jax import lax
from jax.sharding import PartitionSpec as P

dilation_rates = (2, 4, 8)
both = ("gy", "gz")


def extended(cells, sides, width):
    for axis, dim in sides:
        count = lax.axis_size(axis)
        ends = count - 1
        head = lax.slice_in_dim(cells, 0, width, axis=dim)
        tail = lax.slice_in_dim(cells, cells.shape[dim] - width, cells.shape[dim], axis=dim)
        cells = jnp.concatenate(
            [
                lax.ppermute(tail, axis, [(i, (i + 1) % count) for i in range(ends)]),
                cells,
                lax.ppermute(head, axis, [((i + 1) % count, i) for i in range(ends)]),
            ],
            axis=dim,
        )
    return cells


def silu_slope(value):
    sigma = jax.nn.sigmoid(value)
    return sigma * (1.0 + value * (1.0 - sigma))


def depth_taps(dilation, depth):
    return [tap for tap in range(3) if abs(tap - 1) * dilation < depth]


def patches(wide, margin, dilation, shape, flip=False):
    depth, rows, cols = shape
    channels = wide.shape[-1]
    deep = jnp.pad(wide, ((dilation, dilation), (0, 0), (0, 0), (0, 0)))
    start = margin - dilation
    pieces = []
    for first in depth_taps(dilation, depth):
        for second in range(3):
            for third in range(3):
                a, b, c = (2 - first, 2 - second, 2 - third) if flip else (first, second, third)
                pieces.append(
                    deep[
                        a * dilation : a * dilation + depth,
                        start + b * dilation : start + b * dilation + rows,
                        start + c * dilation : start + c * dilation + cols,
                    ].reshape(-1, channels)
                )
    return jnp.concatenate(pieces, axis=1)


def dot32(lhs, rhs):
    return jnp.dot(lhs, rhs, preferred_element_type=jnp.float32)


def outer(lhs, rhs):
    return lax.dot_general(lhs, rhs, (((0,), (0,)), ((), ())), preferred_element_type=jnp.float32)


def bit_list(axis):
    return [(axis, bit) for bit in range(int(math.log2(lax.axis_size(axis))))]


def share_of(terms, order):
    sizes = {axis: lax.axis_size(axis) for axis in both}
    dims = [(axis, bit) for axis in both for bit in reversed(range(int(math.log2(sizes[axis]))))]
    held = terms.reshape((2,) * len(dims) + terms.shape[1:])
    left = list(dims)
    for step, (axis, bit) in enumerate(order):
        at = left.index((axis, bit))
        mine = (lax.axis_index(axis) >> bit) & 1
        low = lax.index_in_dim(held, 0, at, keepdims=False)
        high = lax.index_in_dim(held, 1, at, keepdims=False)
        keep = jnp.where(mine == 0, low, high)
        send = jnp.where(mine == 0, high, low)
        got = lax.ppermute(send, axis, [(i, i ^ (1 << bit)) for i in range(sizes[axis])])
        held = keep.astype(jnp.float32) + got.astype(jnp.float32)
        left.pop(at)
        if step < len(order) - 1:
            held = held.astype(jnp.bfloat16)
    return held


def spread(packed, runs, final_rows):
    ngy, ngz = lax.axis_size("gy"), lax.axis_size("gz")
    count = ngy * ngz
    rows = packed.shape[0]
    edges = []
    for start, target, length in runs:
        for source in range(count):
            lo, hi = max(start, source * rows), min(start + length, source * rows + rows)
            shift = target - start
            if lo >= hi:
                continue
            for owner in range((lo + shift) // final_rows, (hi - 1 + shift) // final_rows + 1):
                cut_lo = max(lo + shift, owner * final_rows) - shift
                cut_hi = min(hi + shift, (owner + 1) * final_rows) - shift
                edges.append((source, owner, cut_lo, cut_hi, shift))
    rounds = []
    for edge in edges:
        for group in rounds:
            if all(edge[0] != other[0] and edge[1] != other[1] for other in group):
                group.append(edge)
                break
        else:
            rounds.append([edge])
    me = lax.axis_index("gy") * ngz + lax.axis_index("gz")
    at = jnp.arange(rows, dtype=jnp.int32)[:, None]
    total = None
    for group in rounds:
        table = np.zeros((count, 3), np.int32)
        table[:, 2] = rows
        pairs = []
        for source, owner, lo, hi, shift in group:
            table[source, 0] = lo - source * rows
            table[source, 1] = hi - source * rows
            table[owner, 2] = rows + source * rows + shift - owner * final_rows
            pairs.append((source, owner))
        line = jnp.asarray(table)[me]
        send = jnp.where((at >= line[0]) & (at < line[1]), packed, 0.0)
        got = lax.ppermute(send, both, pairs)
        room = jnp.zeros((final_rows + 2 * rows, packed.shape[1]), packed.dtype)
        room = lax.dynamic_update_slice(room, got, (line[2], 0))[rows : rows + final_rows]
        total = room if total is None else total + room
    return total


def local(volume, block_weight, aspp_weight, proj_weight, cotangent):
    shape = volume.shape[:3]
    depth, row_count, col_count = shape
    channels = volume.shape[-1]
    branch_width = aspp_weight.shape[-1]
    widest_rate = max(dilation_rates)
    count = lax.axis_size("gy") * lax.axis_size("gz")
    sides = (("gy", 1), ("gz", 2))
    gy_bits, gz_bits = bit_list("gy"), bit_list("gz")

    taps = [depth_taps(dilation, depth) for dilation in dilation_rates]
    branch_weights = [
        aspp_weight[branch, taps[branch][0] : taps[branch][-1] + 1].reshape(-1, channels, branch_width)
        for branch in range(len(dilation_rates))
    ]
    back_weight = jnp.concatenate(
        [jnp.swapaxes(weight, 1, 2).reshape(-1, channels) for weight in branch_weights]
    )
    block_back = jnp.swapaxes(block_weight.reshape(-1, channels, channels), 1, 2).reshape(-1, channels)

    volume_taps = patches(extended(volume, sides, 1), 1, 1, shape)
    pre_block = dot32(volume_taps, block_weight.reshape(-1, channels))
    hidden = jax.nn.silu(pre_block).astype(jnp.bfloat16)
    hidden_wide = extended(hidden.reshape(*shape, channels), sides, widest_rate)
    hidden_taps = [patches(hidden_wide, widest_rate, dilation, shape) for dilation in dilation_rates]
    branch_pre = jnp.concatenate(
        [
            dot32(rows, weight.reshape(-1, branch_width))
            for rows, weight in zip(hidden_taps, branch_weights)
        ],
        -1,
    )
    joined = jax.nn.silu(branch_pre).astype(jnp.bfloat16)
    pyramid_out = dot32(joined, proj_weight).reshape(*shape, branch_width).astype(jnp.bfloat16)
    grad_rows = cotangent.reshape(-1, branch_width)
    proj_back = lax.dot_general(
        grad_rows, proj_weight, (((1,), (1,)), ((), ())), preferred_element_type=jnp.float32
    )
    grad_joined = (proj_back * silu_slope(branch_pre)).astype(jnp.bfloat16)
    grad_wide = extended(grad_joined.reshape(*shape, -1), sides, widest_rate)

    grad_proj = outer(joined, grad_rows).astype(jnp.bfloat16).reshape(count, -1, branch_width)
    grad_aspp = jnp.concatenate(
        [
            outer(rows, grad_joined[:, branch * branch_width : (branch + 1) * branch_width]).astype(jnp.bfloat16)
            for branch, rows in enumerate(hidden_taps)
        ]
    ).reshape(count, -1, branch_width)
    packed_rows = grad_aspp.shape[1]
    packed = share_of(jnp.concatenate([grad_aspp, grad_proj], 1), gy_bits[:1] + gz_bits + gy_bits[:0:-1])
    proj_share = packed[packed_rows:].reshape(-1)
    runs, start = [], 0
    for branch in range(len(dilation_rates)):
        length = len(taps[branch]) * 9 * channels
        runs.append((start, (branch * 27 + taps[branch][0] * 9) * channels, length))
        start += length
    aspp_share = spread(
        packed[:packed_rows], runs, len(dilation_rates) * 27 * channels // count
    ).reshape(-1)

    grad_taps = jnp.concatenate(
        [
            patches(
                grad_wide[..., branch * branch_width : (branch + 1) * branch_width],
                widest_rate,
                dilation,
                shape,
                flip=True,
            )
            for branch, dilation in enumerate(dilation_rates)
        ],
        1,
    )
    grad_hidden = dot32(grad_taps, back_weight)
    grad_pre = (grad_hidden * silu_slope(pre_block)).astype(jnp.bfloat16)
    grad_pre_rim = extended(grad_pre.reshape(*shape, channels), sides, 1)

    grad_block = outer(volume_taps, grad_pre).astype(jnp.bfloat16).reshape(count, -1, channels)
    half = grad_block.shape[1] // 2
    block_share = jnp.concatenate(
        [
            share_of(grad_block[:, :half], gy_bits[:1] + gz_bits + gy_bits[:0:-1]),
            share_of(grad_block[:, half:], gy_bits[:1] + gz_bits[::-1] + gy_bits[:0:-1]),
        ]
    ).reshape(-1)
    grad_volume = dot32(patches(grad_pre_rim, 1, 1, shape, flip=True), block_back)
    grad_volume = grad_volume.reshape(*shape, channels).astype(jnp.bfloat16)
    return (pyramid_out, grad_volume, block_share, aspp_share, proj_share)


def solution(mesh):
    in_specs = (P(None, "gy", "gz", None), P(), P(), P(), P(None, "gy", "gz", None))
    out_specs = (
        P(None, "gy", "gz", None),
        P(None, "gy", "gz", None),
        P(("gy", "gz")),
        P(("gy", "gz")),
        P(("gy", "gz")),
    )
    return jax.shard_map(local, mesh=mesh, in_specs=in_specs, out_specs=out_specs, check_vma=False)
```

time: 494 us -> 236 us (0.48)
  waiting for transfers between devices: 282 us -> 91.2 us
  matrix products: 80.6 us -> 14.4 us
  starting transfers between devices: 78.1 us -> 55 us
  other arithmetic: 11.9 us -> 26.3 us
  local copies, waits for them, and re-layouts: 23.7 us -> 37.5 us
  between operations: 16.9 us -> 8.37 us
    unnamed x2 -> x0, waiting for transfers between devices: 271 us -> none
    dot_general x293 -> x13, matrix products: 80.6 us -> 14.4 us  [the longest x7 7.79 us: dot32(): return jnp.dot(lhs, rhs, preferred_element_type=jnp.float32)]
    ppermute x0 -> x18, waiting for transfers between devices: none -> 57.8 us  [the longest x15 53.6 us: share_of(): lax.ppermute(send, axis, [(i, i ^ 1 << bit) for i in range(sizes[axis])])]
    ppermute x12 -> x8, starting transfers between devices: 62.5 us -> 27.8 us  [extended(): lax.ppermute(tail, axis, [(i, (i + 1) % count) for i in range(ends)])]
    ppermute x12 -> x8, waiting for transfers between devices: 7.28 us -> 25.7 us  [extended(): lax.ppermute(head, axis, [((i + 1) % count, i) for i in range(ends)])]
    ppermute x0 -> x18, starting transfers between devices: none -> 16.4 us  [the longest x15 13.8 us: share_of(): lax.ppermute(send, axis, [(i, i ^ 1 << bit) for i in range(sizes[axis])])]
    slice x11 -> x16, local copies, waits for them, and re-layouts: 1.69 us -> 13 us  [the longest x5 7.34 us: local(): aspp_weight[branch, taps[branch][0]:taps[branch][-1] + 1]]
    concatenate x11 -> x14, other arithmetic: 2.51 us -> 11.5 us  [extended(): jnp.concatenate([lax.ppermute(tail, axis, [(i, (i + 1) % count) for i in...]
  transfers between devices with their start and end apart: 25 -> 34, of which waited for: 6 -> 16; matrix products, arithmetic and copies ran while one was open for 11% -> 22% of each run, Pallas kernels for 0% -> 0%
where the time goes in v1:
time: 236 us; the launch traced here: 233 us
  waiting for transfers between devices  91.2 us (39%)
  starting transfers between devices  55 us (23%)
  local copies, waits for them, and re-layouts  37.5 us (16%)
  other arithmetic  26.3 us (11%)
  matrix products  14.4 us (6%)
  between operations  8.37 us (4%)
    ppermute x15, waiting for transfers between devices, share_of(): lax.ppermute(send, axis, [(i, i ^ 1 << bit) for i in range(sizes[axis])])  53.6 us
    ppermute x8, starting transfers between devices, extended(): lax.ppermute(tail, axis, [(i, (i + 1) % count) for i in range(ends)])  27.8 us
    ppermute x8, waiting for transfers between devices, extended(): lax.ppermute(head, axis, [((i + 1) % count, i) for i in range(ends)])  25.7 us
    ppermute x15, starting transfers between devices, share_of(): lax.ppermute(send, axis, [(i, i ^ 1 << bit) for i in range(sizes[axis])])  13.8 us
    concatenate x14, other arithmetic, extended(): jnp.concatenate([lax.ppermute(tail, axis, [(i, (i + 1) % count) for i in...  11.5 us
    ppermute x8, starting transfers between devices, extended(): lax.ppermute(head, axis, [((i + 1) % count, i) for i in range(ends)])  10.7 us
    dot_general x7, matrix products, dot32(): return jnp.dot(lhs, rhs, preferred_element_type=jnp.float32)  7.79 us
    ppermute x8, waiting for transfers between devices, extended(): lax.ppermute(tail, axis, [(i, (i + 1) % count) for i in range(ends)])  7.72 us
  transfers between devices with their start and end apart: 34, of which 16 were waited for; matrix products, arithmetic and copies ran while one was open for 22% of the time, Pallas kernels for 0%

profile of v1, /device:TPU:0, one launch (start us, length us, event | category | flops | bytes accessed | tf_op | source)
XLA Modules:
  0.0 232.8 jit_solution(16016944140757205863)
XLA Ops:
  1.4 2.3 %collective-permute-start = (bf16[4,1,8,256]{3,2,1,0:T(8,128)(2,1)S(1)}, bf16[4,1,8,256]{3,2,1,0:T(8,128)(2,1)S(1)}, u32[]{:S(2)}, u32[]{:S(2)}) collective-permute-start(bf16[4,1,8,256]{3,2,1,0:T(8,128)(2,1)S(1)} %get-tuple-element.149), channel_id=1, source_target_pairs={{0,4},{4,8},{8,12},{12,16},{16,20},{20,24},{24,28},{1,5},{5,9},{9,... | collective-permute-start | bytes 49160 | tf_op jit(solution)/shard_map/ppermute | solution.py:21
  3.8 1.3 collective-permute-start.1
  5.1 1.3 fusion.58
  10.2 3.4 %collective-permute-start.2 = (bf16[4,10,1,256]{3,2,1,0:T(2,128)(2,1)S(1)}, bf16[4,10,1,256]{3,2,1,0:T(2,128)(2,1)S(1)}, u32[]{:S(2)}, u32[]{:S(2)}) collective-permute-start(bf16[4,10,1,256]{3,2,1,0:T(2,128)(2,1)S(1)} %get-tuple-element.136), channel_id=1, source_target_pairs={{0,1},{1,2},{2,3},{4,5},{5,6},{6,7},{8,9},{9,10},{10,11},{12,13},{... | collective-permute-start | bytes 61448 | tf_op jit(solution)/shard_map/ppermute | solution.py:21
  13.6 1.3 collective-permute-start.3
  15.5 4.0 %collective-permute-done.3 = bf16[4,10,1,256]{3,2,1,0:T(2,128)(2,1)S(1)} collective-permute-done((bf16[4,10,1,256]{3,2,1,0:T(2,128)(2,1)S(1)}, bf16[4,10,1,256]{3,2,1,0:T(2,128)(2,1)S(1)}, u32[]{:S(2)}, u32[]{:S(2)}) %collective-permute-start.3) | collective-permute-done | bytes 20512 | tf_op jit(solution)/shard_map/ppermute | solution.py:23
  22.3 1.8 multiply_convert_fusion.1
  24.1 2.9 %collective-permute-start.4 = (bf16[4,8,8,256]{3,2,1,0:T(8,128)(2,1)S(1)}, bf16[4,8,8,256]{3,2,1,0:T(8,128)(2,1)S(1)}, u32[]{:S(2)}, u32[]{:S(2)}) collective-permute-start(bf16[4,8,8,256]{3,2,1,0:T(8,128)(2,1)S(1)} %bitcast.322), channel_id=1, source_target_pairs={{0,4},{4,8},{8,12},{12,16},{16,20},{20,24},{24,28},{1,5},{5,9},{9,... | collective-permute-start | bytes 393224 | tf_op jit(solution)/shard_map/ppermute | solution.py:21
  27.1 1.3 collective-permute-start.5
  29.7 2.9 %collective-permute-done.5 = bf16[4,8,8,256]{3,2,1,0:T(8,128)(2,1)S(1)} collective-permute-done((bf16[4,8,8,256]{3,2,1,0:T(8,128)(2,1)S(1)}, bf16[4,8,8,256]{3,2,1,0:T(8,128)(2,1)S(1)}, u32[]{:S(2)}, u32[]{:S(2)}) %collective-permute-start.5) | collective-permute-done | bytes 131104 | tf_op jit(solution)/shard_map/ppermute | solution.py:23
  33.4 5.0 %collective-permute-start.6 = (bf16[4,24,8,256]{3,2,1,0:T(8,128)(2,1)}, bf16[4,24,8,256]{3,2,1,0:T(8,128)(2,1)}, u32[]{:S(2)}, u32[]{:S(2)}) collective-permute-start(bf16[4,24,8,256]{3,2,1,0:T(8,128)(2,1)} %pad_maximum_fusion.4), channel_id=1, source_target_pairs={{0,1},{1,2},{2,3},{4,5},{5,6},{6,7},{8,9},{9,10},{10,11},{12,13},{... | collective-permute-start | bytes 1179656 | tf_op jit(solution)/shard_map/ppermute | solution.py:21
  39.8 1.3 fusion.55
  41.1 1.6 slice.856
  48.7 2.3 copy.103
  51.0 5.8 %copy.106 = bf16[27,256,256]{2,1,0:T(8,128)(2,1)} copy(bf16[27,256,256]{1,2,0:T(8,128)(2,1)} %bitcast.319) | data formatting | bytes 7077888 | tf_op jit(solution)/shard_map/transpose | solution.py:153
  62.3 1.5 pad_maximum_fusion.2
  65.5 1.3 select_maximum_fusion
  68.1 1.3 fusion.74
  70.9 2.3 %convolution_convert_fusion.1 = bf16[6912,128]{1,0:T(8,128)(2,1)} fusion(bf16[256,6912]{1,0:T(8,128)(2,1)S(1)} %constant_dynamic-update-slice_fusion.30, bf16[256,384]{0,1:T(8,128)(2,1)S(1)} %fusion.23), kind=kOutput, calls=%fused_computation.1 | convolution fusion | flops 453869568 | bytes 5373952 | tf_op jit(solution)/shard_map/dot_general | solution.py:64
  73.2 1.3 convolution_convert_fusion.3
  74.6 1.4 convolution_convert_fusion.2
  76.9 5.3 %collective-permute-start.8 = (bf16[4,8,8,384]{3,2,1,0:T(8,128)(2,1)S(1)}, bf16[4,8,8,384]{3,2,1,0:T(8,128)(2,1)S(1)}, u32[]{:S(2)}, u32[]{:S(2)}) collective-permute-start(bf16[4,8,8,384]{3,2,1,0:T(8,128)(2,1)S(1)} %bitcast.300), channel_id=1, source_target_pairs={{0,4},{4,8},{8,12},{12,16},{16,20},{20,24},{24,28},{1,5},{5,9},{9,... | collective-permute-start | bytes 589832 | tf_op jit(solution)/shard_map/ppermute | solution.py:21
  82.3 1.5 collective-permute-start.9
  83.7 3.8 %pad_maximum_fusion = bf16[11520,128]{1,0:T(8,128)(2,1)S(1)} fusion(bf16[2304,128]{1,0:T(8,128)(2,1)} %convolution_convert_fusion.2, bf16[2304,128]{1,0:T(8,128)(2,1)} %convolution_convert_fusion.3, bf16[6912,128]{1,0:T(8,128)(2,1)} %convolution_convert_fusion.1), kind=kLoop, calls=%fused_computation.19 | loop fusion | flops 8847360 | bytes 5898240 | tf_op jit(solution)/shard_map/concatenate | solution.py:177
  90.6 4.3 %collective-permute-start.10 = (bf16[4,24,8,384]{3,2,1,0:T(8,128)(2,1)S(1)}, bf16[4,24,8,384]{3,2,1,0:T(8,128)(2,1)S(1)}, u32[]{:S(2)}, u32[]{:S(2)}) collective-permute-start(bf16[4,24,8,384]{3,2,1,0:T(8,128)(2,1)S(1)} %pad_maximum_fusion.3), channel_id=1, source_target_pairs={{0,1},{1,2},{2,3},{4,5},{5,6},{6,7},{8,9},{9,10},{10,11},{12,13},{... | collective-permute-start | bytes 1769480 | tf_op jit(solution)/shard_map/ppermute | solution.py:21
  96.4 1.6 copy.121
  100.7 7.7 %collective-permute-done.10 = bf16[4,24,8,384]{3,2,1,0:T(8,128)(2,1)S(1)} collective-permute-done((bf16[4,24,8,384]{3,2,1,0:T(8,128)(2,1)S(1)}, bf16[4,24,8,384]{3,2,1,0:T(8,128)(2,1)S(1)}, u32[]{:S(2)}, u32[]{:S(2)}) %collective-permute-start.10) | collective-permute-done | bytes 589856 | tf_op jit(solution)/shard_map/ppermute | solution.py:21
  108.4 13.8 %collective-permute-done.11 = bf16[4,24,8,384]{3,2,1,0:T(8,128)(2,1)S(1)} collective-permute-done((bf16[4,24,8,384]{3,2,1,0:T(8,128)(2,1)S(1)}, bf16[4,24,8,384]{3,2,1,0:T(8,128)(2,1)S(1)}, u32[]{:S(2)}, u32[]{:S(2)}) %collective-permute-start.11) | collective-permute-done | bytes 589856 | tf_op jit(solution)/shard_map/ppermute | solution.py:23
  132.7 2.3 collective-permute-start.12
  136.5 2.7 %collective-permute-done.13 = bf16[4,1,8,256]{3,2,1,0:T(8,128)(2,1)S(1)} collective-permute-done((bf16[4,1,8,256]{3,2,1,0:T(8,128)(2,1)S(1)}, bf16[4,1,8,256]{3,2,1,0:T(8,128)(2,1)S(1)}, u32[]{:S(2)}, u32[]{:S(2)}) %collective-permute-start.13) | collective-permute-done | bytes 16416 | tf_op jit(solution)/shard_map/ppermute | solution.py:23
  139.2 2.2 collective-permute-start.14
  141.4 1.5 collective-permute-start.15
  144.0 2.3 collective-permute-start.21
  149.9 1.7 convolution_convert_fusion.4
  152.8 1.4 collective-permute-start.27
  156.8 25.7 %collective-permute-done.17 = bf16[2,2,2,108,256]{4,3,2,1,0:T(8,128)(2,1)S(1)} collective-permute-done((bf16[2,2,2,108,256]{4,3,2,1,0:T(8,128)(2,1)S(1)}, bf16[2,2,2,108,256]{4,3,2,1,0:T(8,128)(2,1)S(1)}, u32[]{:S(2)}, u32[]{:S(2)}) %collective-permute-start.17) | collective-permute-done | bytes 442400 | tf_op jit(solution)/shard_map/ppermute | solution.py:83
  184.8 2.1 collective-permute-start.28
  186.8 4.4 %collective-permute-done.18 = bf16[2,2,108,256]{3,2,1,0:T(8,128)(2,1)S(1)} collective-permute-done((bf16[2,2,108,256]{3,2,1,0:T(8,128)(2,1)S(1)}, bf16[2,2,108,256]{3,2,1,0:T(8,128)(2,1)S(1)}, u32[]{:S(2)}, u32[]{:S(2)}) %collective-permute-start.18) | collective-permute-done | bytes 221216 | tf_op jit(solution)/shard_map/ppermute | solution.py:83
  191.3 2.5 %collective-permute-start.19 = (bf16[2,108,256]{2,1,0:T(8,128)(2,1)S(1)}, bf16[2,108,256]{2,1,0:T(8,128)(2,1)S(1)}, u32[]{:S(2)}, u32[]{:S(2)}) collective-permute-start(bf16[2,108,256]{2,1,0:T(8,128)(2,1)S(1)} %select_bitcast_fusion.9), channel_id=1, source_target_pairs={{0,16},{4,20},{8,24},{12,28},{16,0},{20,4},{24,8},{28,12},{1,17},{... | collective-permute-start | bytes 331784 | tf_op jit(solution)/shard_map/ppermute | solution.py:83
  194.5 6.4 %collective-permute-done.19 = bf16[2,108,256]{2,1,0:T(8,128)(2,1)S(1)} collective-permute-done((bf16[2,108,256]{2,1,0:T(8,128)(2,1)S(1)}, bf16[2,108,256]{2,1,0:T(8,128)(2,1)S(1)}, u32[]{:S(2)}, u32[]{:S(2)}) %collective-permute-start.19) | collective-permute-done | bytes 110624 | tf_op jit(solution)/shard_map/ppermute | solution.py:83
  201.1 1.8 collective-permute-done.24
  203.2 2.3 collective-permute-done.20
  205.9 1.9 collective-permute-done.25
  207.8 7.4 %collective-permute-done.29 = bf16[2,372,128]{2,1,0:T(8,128)(2,1)S(1)} collective-permute-done((bf16[2,372,128]{2,1,0:T(8,128)(2,1)S(1)}, bf16[2,372,128]{2,1,0:T(8,128)(2,1)S(1)}, u32[]{:S(2)}, u32[]{:S(2)}) %collective-permute-start.29) | collective-permute-done | bytes 190496 | tf_op jit(solution)/shard_map/ppermute | solution.py:83
  216.2 3.7 %collective-permute-done.30 = bf16[372,128]{1,0:T(8,128)(2,1)S(1)} collective-permute-done((bf16[372,128]{1,0:T(8,128)(2,1)S(1)}, bf16[372,128]{1,0:T(8,128)(2,1)S(1)}, u32[]{:S(2)}, u32[]{:S(2)}) %collective-permute-start.30) | collective-permute-done | bytes 95264 | tf_op jit(solution)/shard_map/ppermute | solution.py:83
  223.5 4.2 %collective-permute-done.32 = f32[360,128]{1,0:T(8,128)S(1)} collective-permute-done((f32[360,128]{1,0:T(8,128)S(1)}, f32[360,128]{1,0:T(8,128)S(1)}, u32[]{:S(2)}, u32[]{:S(2)}) %collective-permute-start.32) | collective-permute-done | bytes 184352 | tf_op jit(solution)/shard_map/ppermute | solution.py:128
  229.1 1.4 dynamic_update_slice.9
  230.6 1.4 dynamic_update_slice.11
  (310 shorter events, 59.4 us)
Async XLA Ops:
  0.6 70.0 %copy-start = (bf16[384,128]{1,0:T(8,128)(2,1)S(1)}, bf16[384,128]{1,0:T(8,128)(2,1)}, u32[]{:S(2)}) copy-start(bf16[384,128]{1,0:T(8,128)(2,1)} %param.11) | copy-start | bytes 294916
  1.4 6.4 %collective-permute-start = (bf16[4,1,8,256]{3,2,1,0:T(8,128)(2,1)S(1)}, bf16[4,1,8,256]{3,2,1,0:T(8,128)(2,1)S(1)}, u32[]{:S(2)}, u32[]{:S(2)}) collective-permute-start(bf16[4,1,8,256]{3,2,1,0:T(8,128)(2,1)S(1)} %get-tuple-element.149), channel_id=1, source_target_pairs={{0,4},{4,8},{8,12},{12,16},{16,20},{20,24},{24,28},{1,5},{5,9},{9,... | collective-permute-start | bytes 49160 | tf_op jit(solution)/shard_map/ppermute | solution.py:21
  3.8 5.3 %collective-permute-start.1 = (bf16[4,1,8,256]{3,2,1,0:T(8,128)(2,1)S(1)}, bf16[4,1,8,256]{3,2,1,0:T(8,128)(2,1)S(1)}, u32[]{:S(2)}, u32[]{:S(2)}) collective-permute-start(bf16[4,1,8,256]{3,2,1,0:T(8,128)(2,1)S(1)} %get-tuple-element.148), channel_id=1, source_target_pairs={{4,0},{8,4},{12,8},{16,12},{20,16},{24,20},{28,24},{5,1},{9,5},{13... | collective-permute-start | bytes 49160 | tf_op jit(solution)/shard_map/ppermute | solution.py:23
  10.2 5.3 %collective-permute-start.2 = (bf16[4,10,1,256]{3,2,1,0:T(2,128)(2,1)S(1)}, bf16[4,10,1,256]{3,2,1,0:T(2,128)(2,1)S(1)}, u32[]{:S(2)}, u32[]{:S(2)}) collective-permute-start(bf16[4,10,1,256]{3,2,1,0:T(2,128)(2,1)S(1)} %get-tuple-element.136), channel_id=1, source_target_pairs={{0,1},{1,2},{2,3},{4,5},{5,6},{6,7},{8,9},{9,10},{10,11},{12,13},{... | collective-permute-start | bytes 61448 | tf_op jit(solution)/shard_map/ppermute | solution.py:21
  13.6 5.9 %collective-permute-start.3 = (bf16[4,10,1,256]{3,2,1,0:T(2,128)(2,1)S(1)}, bf16[4,10,1,256]{3,2,1,0:T(2,128)(2,1)S(1)}, u32[]{:S(2)}, u32[]{:S(2)}) collective-permute-start(bf16[4,10,1,256]{3,2,1,0:T(2,128)(2,1)S(1)} %get-tuple-element.137), channel_id=1, source_target_pairs={{1,0},{2,1},{3,2},{5,4},{6,5},{7,6},{9,8},{10,9},{11,10},{13,12},{... | collective-permute-start | bytes 61448 | tf_op jit(solution)/shard_map/ppermute | solution.py:23
  20.2 2.2 copy-start.5
  21.1 3.0 %copy-start.3 = (bf16[256,6912]{1,0:T(8,128)(2,1)}, bf16[256,6912]{1,0:T(8,128)(2,1)S(1)}, u32[]{:S(2)}) copy-start(bf16[256,6912]{1,0:T(8,128)(2,1)S(1)} %constant_dynamic-update-slice_fusion.3) | copy-start | bytes 10616836
  24.1 17.0 %copy-start.8 = (bf16[256,256]{1,0:T(8,128)(2,1)}, bf16[256,256]{1,0:T(8,128)(2,1)S(1)}, u32[]{:S(2)}) copy-start(bf16[256,256]{1,0:T(8,128)(2,1)S(1)} %get-tuple-element.159) | copy-start | bytes 393220
  24.1 5.6 %collective-permute-start.4 = (bf16[4,8,8,256]{3,2,1,0:T(8,128)(2,1)S(1)}, bf16[4,8,8,256]{3,2,1,0:T(8,128)(2,1)S(1)}, u32[]{:S(2)}, u32[]{:S(2)}) collective-permute-start(bf16[4,8,8,256]{3,2,1,0:T(8,128)(2,1)S(1)} %bitcast.322), channel_id=1, source_target_pairs={{0,4},{4,8},{8,12},{12,16},{16,20},{20,24},{24,28},{1,5},{5,9},{9,... | collective-permute-start | bytes 393224 | tf_op jit(solution)/shard_map/ppermute | solution.py:21
  27.1 5.5 %collective-permute-start.5 = (bf16[4,8,8,256]{3,2,1,0:T(8,128)(2,1)S(1)}, bf16[4,8,8,256]{3,2,1,0:T(8,128)(2,1)S(1)}, u32[]{:S(2)}, u32[]{:S(2)}) collective-permute-start(bf16[4,8,8,256]{3,2,1,0:T(8,128)(2,1)S(1)} %bitcast.323), channel_id=1, source_target_pairs={{4,0},{8,4},{12,8},{16,12},{20,16},{24,20},{28,24},{5,1},{9,5},{13... | collective-permute-start | bytes 393224 | tf_op jit(solution)/shard_map/ppermute | solution.py:23
  29.7 10.1 %copy-start.10 = (bf16[4,8,8,256]{3,2,1,0:T(8,128)(2,1)}, bf16[4,8,8,256]{3,2,1,0:T(8,128)(2,1)S(1)}, u32[]{:S(2)}) copy-start(bf16[4,8,8,256]{3,2,1,0:T(8,128)(2,1)S(1)} %collective-permute-done.4) | copy-start | bytes 393220
  32.6 7.2 %copy-start.6 = (bf16[4,8,8,256]{3,2,1,0:T(8,128)(2,1)}, bf16[4,8,8,256]{3,2,1,0:T(8,128)(2,1)S(1)}, u32[]{:S(2)}) copy-start(bf16[4,8,8,256]{3,2,1,0:T(8,128)(2,1)S(1)} %collective-permute-done.5) | copy-start | bytes 393220
  33.4 28.9 %collective-permute-start.6 = (bf16[4,24,8,256]{3,2,1,0:T(8,128)(2,1)}, bf16[4,24,8,256]{3,2,1,0:T(8,128)(2,1)}, u32[]{:S(2)}, u32[]{:S(2)}) collective-permute-start(bf16[4,24,8,256]{3,2,1,0:T(8,128)(2,1)} %pad_maximum_fusion.4), channel_id=1, source_target_pairs={{0,1},{1,2},{2,3},{4,5},{5,6},{6,7},{8,9},{9,10},{10,11},{12,13},{... | collective-permute-start | bytes 1179656 | tf_op jit(solution)/shard_map/ppermute | solution.py:21
  38.5 23.8 %collective-permute-start.7 = (bf16[4,24,8,256]{3,2,1,0:T(8,128)(2,1)}, bf16[4,24,8,256]{3,2,1,0:T(8,128)(2,1)S(1)}, u32[]{:S(2)}, u32[]{:S(2)}) collective-permute-start(bf16[4,24,8,256]{3,2,1,0:T(8,128)(2,1)} %pad_maximum_fusion.4), channel_id=1, source_target_pairs={{1,0},{2,1},{3,2},{5,4},{6,5},{7,6},{9,8},{10,9},{11,10},{13,12},{... | collective-permute-start | bytes 1179656 | tf_op jit(solution)/shard_map/ppermute | solution.py:23
  62.3 3.2 %copy-start.7 = (bf16[4,8,8,256]{3,2,1,0:T(8,128)(2,1)S(1)}, bf16[4,8,8,256]{3,2,1,0:T(8,128)(2,1)}, u32[]{:S(2)}) copy-start(bf16[4,8,8,256]{3,2,1,0:T(8,128)(2,1)} %copy-done.6) | copy-start | bytes 393220
  62.3 3.2 %copy-start.9 = (bf16[256,256]{1,0:T(8,128)(2,1)S(1)}, bf16[256,256]{1,0:T(8,128)(2,1)}, u32[]{:S(2)}) copy-start(bf16[256,256]{1,0:T(8,128)(2,1)} %copy-done.8) | copy-start | bytes 393220
  62.3 3.2 %copy-start.11 = (bf16[4,8,8,256]{3,2,1,0:T(8,128)(2,1)S(1)}, bf16[4,8,8,256]{3,2,1,0:T(8,128)(2,1)}, u32[]{:S(2)}) copy-start(bf16[4,8,8,256]{3,2,1,0:T(8,128)(2,1)} %copy-done.10) | copy-start | bytes 393220
  76.9 10.6 %copy-start.13 = (bf16[256,384]{0,1:T(8,128)(2,1)S(1)}, bf16[256,384]{0,1:T(8,128)(2,1)}, u32[]{:S(2)}) copy-start(bf16[256,384]{0,1:T(8,128)(2,1)} %multiply_convert_fusion) | copy-start | bytes 589828
  76.9 10.6 %copy-start.19 = (bf16[4,8,8,128]{3,2,1,0:T(8,128)(2,1)S(1)}, bf16[4,8,8,128]{3,2,1,0:T(8,128)(2,1)}, u32[]{:S(2)}) copy-start(bf16[4,8,8,128]{3,2,1,0:T(8,128)(2,1)} %param.12) | copy-start | bytes 196612
  76.9 12.6 %collective-permute-start.8 = (bf16[4,8,8,384]{3,2,1,0:T(8,128)(2,1)S(1)}, bf16[4,8,8,384]{3,2,1,0:T(8,128)(2,1)S(1)}, u32[]{:S(2)}, u32[]{:S(2)}) collective-permute-start(bf16[4,8,8,384]{3,2,1,0:T(8,128)(2,1)S(1)} %bitcast.300), channel_id=1, source_target_pairs={{0,4},{4,8},{8,12},{12,16},{16,20},{20,24},{24,28},{1,5},{5,9},{9,... | collective-permute-start | bytes 589832 | tf_op jit(solution)/shard_map/ppermute | solution.py:21
  82.3 7.3 %collective-permute-start.9 = (bf16[4,8,8,384]{3,2,1,0:T(8,128)(2,1)S(1)}, bf16[4,8,8,384]{3,2,1,0:T(8,128)(2,1)}, u32[]{:S(2)}, u32[]{:S(2)}) collective-permute-start(bf16[4,8,8,384]{3,2,1,0:T(8,128)(2,1)S(1)} %bitcast.301), channel_id=1, source_target_pairs={{4,0},{8,4},{12,8},{16,12},{20,16},{24,20},{28,24},{5,1},{9,5},{13... | collective-permute-start | bytes 589832 | tf_op jit(solution)/shard_map/ppermute | solution.py:23
  90.6 17.8 %collective-permute-start.10 = (bf16[4,24,8,384]{3,2,1,0:T(8,128)(2,1)S(1)}, bf16[4,24,8,384]{3,2,1,0:T(8,128)(2,1)S(1)}, u32[]{:S(2)}, u32[]{:S(2)}) collective-permute-start(bf16[4,24,8,384]{3,2,1,0:T(8,128)(2,1)S(1)} %pad_maximum_fusion.3), channel_id=1, source_target_pairs={{0,1},{1,2},{2,3},{4,5},{5,6},{6,7},{8,9},{9,10},{10,11},{12,13},{... | collective-permute-start | bytes 1769480 | tf_op jit(solution)/shard_map/ppermute | solution.py:21
  94.9 27.3 %collective-permute-start.11 = (bf16[4,24,8,384]{3,2,1,0:T(8,128)(2,1)S(1)}, bf16[4,24,8,384]{3,2,1,0:T(8,128)(2,1)S(1)}, u32[]{:S(2)}, u32[]{:S(2)}) collective-permute-start(bf16[4,24,8,384]{3,2,1,0:T(8,128)(2,1)S(1)} %pad_maximum_fusion.3), channel_id=1, source_target_pairs={{1,0},{2,1},{3,2},{5,4},{6,5},{7,6},{9,8},{10,9},{11,10},{13,12},{... | collective-permute-start | bytes 1769480 | tf_op jit(solution)/shard_map/ppermute | solution.py:23
  96.2 2.7 %copy-start.14 = (bf16[256,384]{0,1:T(8,128)(2,1)S(1)}, bf16[256,384]{0,1:T(8,128)(2,1)}, u32[]{:S(2)}) copy-start(bf16[256,384]{0,1:T(8,128)(2,1)} %multiply_convert_fusion) | copy-start | bytes 589828
  98.0 53.6 %collective-permute-start.26 = (bf16[2,2,2,2,372,128]{5,3,4,2,1,0:T(2,128)(2,1)S(1)}, bf16[2,2,2,2,372,128]{5,3,4,2,1,0:T(2,128)(2,1)S(1)}, u32[]{:S(2)}, u32[]{:S(2)}) collective-permute-start(bf16[2,2,2,2,372,128]{5,3,4,2,1,0:T(2,128)(2,1)S(1)} %copy.121), channel_id=1, source_target_pairs={{0,4},{4,0},{8,12},{12,8},{16,20},{20,16},{24,28},{28,24},{1,5},{5... | collective-permute-start | bytes 4571144 | tf_op jit(solution)/shard_map/ppermute | solution.py:83
  127.6 2.0 copy-start.4
  132.5 21.6 %collective-permute-start.16 = (bf16[2,2,2,2,108,256]{5,3,4,2,1,0:T(2,128)(2,1)S(1)}, bf16[2,2,2,2,108,256]{5,3,4,2,1,0:T(2,128)(2,1)S(1)}, u32[]{:S(2)}, u32[]{:S(2)}) collective-permute-start(bf16[2,2,2,2,108,256]{5,3,4,2,1,0:T(2,128)(2,1)S(1)} %copy.109), channel_id=1, source_target_pairs={{0,4},{4,0},{8,12},{12,8},{16,20},{20,16},{24,28},{28,24},{1,5},{5... | collective-permute-start | bytes 2654216 | tf_op jit(solution)/shard_map/ppermute | solution.py:83
  132.7 3.7 %collective-permute-start.12 = (bf16[4,1,8,256]{3,2,1,0:T(8,128)(2,1)S(1)}, bf16[4,1,8,256]{3,2,1,0:T(8,128)(2,1)S(1)}, u32[]{:S(2)}, u32[]{:S(2)}) collective-permute-start(bf16[4,1,8,256]{3,2,1,0:T(8,128)(2,1)S(1)} %get-tuple-element.138), channel_id=1, source_target_pairs={{0,4},{4,8},{8,12},{12,16},{16,20},{20,24},{24,28},{1,5},{5,9},{9,... | collective-permute-start | bytes 49160 | tf_op jit(solution)/shard_map/ppermute | solution.py:21
  135.0 4.1 %collective-permute-start.13 = (bf16[4,1,8,256]{3,2,1,0:T(8,128)(2,1)S(1)}, bf16[4,1,8,256]{3,2,1,0:T(8,128)(2,1)S(1)}, u32[]{:S(2)}, u32[]{:S(2)}) collective-permute-start(bf16[4,1,8,256]{3,2,1,0:T(8,128)(2,1)S(1)} %get-tuple-element.139), channel_id=1, source_target_pairs={{4,0},{8,4},{12,8},{16,12},{20,16},{24,20},{28,24},{5,1},{9,5},{13... | collective-permute-start | bytes 49160 | tf_op jit(solution)/shard_map/ppermute | solution.py:23
  139.2 7.0 %collective-permute-start.14 = (bf16[4,10,1,256]{3,2,1,0:T(2,128)(2,1)S(1)}, bf16[4,10,1,256]{3,2,1,0:T(2,128)(2,1)S(1)}, u32[]{:S(2)}, u32[]{:S(2)}) collective-permute-start(bf16[4,10,1,256]{3,2,1,0:T(2,128)(2,1)S(1)} %get-tuple-element.131), channel_id=1, source_target_pairs={{0,1},{1,2},{2,3},{4,5},{5,6},{6,7},{8,9},{9,10},{10,11},{12,13},{... | collective-permute-start | bytes 61448 | tf_op jit(solution)/shard_map/ppermute | solution.py:21
  141.4 5.9 %collective-permute-start.15 = (bf16[4,10,1,256]{3,2,1,0:T(2,128)(2,1)S(1)}, bf16[4,10,1,256]{3,2,1,0:T(2,128)(2,1)S(1)}, u32[]{:S(2)}, u32[]{:S(2)}) collective-permute-start(bf16[4,10,1,256]{3,2,1,0:T(2,128)(2,1)S(1)} %get-tuple-element.132), channel_id=1, source_target_pairs={{1,0},{2,1},{3,2},{5,4},{6,5},{7,6},{9,8},{10,9},{11,10},{13,12},{... | collective-permute-start | bytes 61448 | tf_op jit(solution)/shard_map/ppermute | solution.py:23
  144.0 11.4 %collective-permute-start.21 = (bf16[2,2,2,2,108,256]{5,3,4,2,1,0:T(2,128)(2,1)S(1)}, bf16[2,2,2,2,108,256]{5,3,4,2,1,0:T(2,128)(2,1)S(1)}, u32[]{:S(2)}, u32[]{:S(2)}) collective-permute-start(bf16[2,2,2,2,108,256]{5,3,4,2,1,0:T(2,128)(2,1)S(1)} %copy.117), channel_id=1, source_target_pairs={{0,4},{4,0},{8,12},{12,8},{16,20},{20,16},{24,28},{28,24},{1,5},{5... | collective-permute-start | bytes 2654216 | tf_op jit(solution)/shard_map/ppermute | solution.py:83
  152.8 31.7 %collective-permute-start.27 = (bf16[2,2,2,372,128]{4,2,3,1,0:T(2,128)(2,1)S(1)}, bf16[2,2,2,372,128]{4,2,3,1,0:T(2,128)(2,1)S(1)}, u32[]{:S(2)}, u32[]{:S(2)}) collective-permute-start(bf16[2,2,2,372,128]{4,2,3,1,0:T(2,128)(2,1)S(1)} %copy.123), channel_id=1, source_target_pairs={{0,1},{1,0},{2,3},{3,2},{4,5},{5,4},{6,7},{7,6},{8,9},{9,8},{10,11... | collective-permute-start | bytes 2285576 | tf_op jit(solution)/shard_map/ppermute | solution.py:83
  154.5 28.0 %collective-permute-start.17 = (bf16[2,2,2,108,256]{4,3,2,1,0:T(8,128)(2,1)S(1)}, bf16[2,2,2,108,256]{4,3,2,1,0:T(8,128)(2,1)S(1)}, u32[]{:S(2)}, u32[]{:S(2)}) collective-permute-start(bf16[2,2,2,108,256]{4,3,2,1,0:T(8,128)(2,1)S(1)} %select_bitcast_fusion.5), channel_id=1, source_target_pairs={{0,1},{1,0},{2,3},{3,2},{4,5},{5,4},{6,7},{7,6},{8,9},{9,8},{10,11... | collective-permute-start | bytes 1327112 | tf_op jit(solution)/shard_map/ppermute | solution.py:83
  155.8 27.2 %collective-permute-start.22 = (bf16[2,2,2,108,256]{4,3,1,0,2:T(8,128)(2,1)S(1)}, bf16[2,2,2,108,256]{4,3,1,0,2:T(8,128)(2,1)S(1)}, u32[]{:S(2)}, u32[]{:S(2)}) collective-permute-start(bf16[2,2,2,108,256]{4,3,1,0,2:T(8,128)(2,1)S(1)} %select_bitcast_fusion.4), channel_id=1, source_target_pairs={{0,2},{1,3},{2,0},{3,1},{4,6},{5,7},{6,4},{7,5},{8,10},{9,11},{10,... | collective-permute-start | bytes 1327112 | tf_op jit(solution)/shard_map/ppermute | solution.py:83
  182.7 8.5 %collective-permute-start.18 = (bf16[2,2,108,256]{3,2,1,0:T(8,128)(2,1)S(1)}, bf16[2,2,108,256]{3,2,1,0:T(8,128)(2,1)S(1)}, u32[]{:S(2)}, u32[]{:S(2)}) collective-permute-start(bf16[2,2,108,256]{3,2,1,0:T(8,128)(2,1)S(1)} %fusion.41), channel_id=1, source_target_pairs={{0,2},{1,3},{2,0},{3,1},{4,6},{5,7},{6,4},{7,5},{8,10},{9,11},{10,... | collective-permute-start | bytes 663560 | tf_op jit(solution)/shard_map/ppermute | solution.py:83
  183.2 10.7 %collective-permute-start.23 = (bf16[2,2,108,256]{3,2,1,0:T(8,128)(2,1)S(1)}, bf16[2,2,108,256]{3,2,1,0:T(8,128)(2,1)S(1)}, u32[]{:S(2)}, u32[]{:S(2)}) collective-permute-start(bf16[2,2,108,256]{3,2,1,0:T(8,128)(2,1)S(1)} %select_bitcast_fusion.6), channel_id=1, source_target_pairs={{0,1},{1,0},{2,3},{3,2},{4,5},{5,4},{6,7},{7,6},{8,9},{9,8},{10,11... | collective-permute-start | bytes 663560 | tf_op jit(solution)/shard_map/ppermute | solution.py:83
  184.8 20.8 %collective-permute-start.28 = (bf16[2,2,372,128]{3,2,1,0:T(8,128)(2,1)S(1)}, bf16[2,2,372,128]{3,2,1,0:T(8,128)(2,1)S(1)}, u32[]{:S(2)}, u32[]{:S(2)}) collective-permute-start(bf16[2,2,372,128]{3,2,1,0:T(8,128)(2,1)S(1)} %fusion.37), channel_id=1, source_target_pairs={{0,2},{1,3},{2,0},{3,1},{4,6},{5,7},{6,4},{7,5},{8,10},{9,11},{10,... | collective-permute-start | bytes 1142792 | tf_op jit(solution)/shard_map/ppermute | solution.py:83
  191.3 9.6 %collective-permute-start.19 = (bf16[2,108,256]{2,1,0:T(8,128)(2,1)S(1)}, bf16[2,108,256]{2,1,0:T(8,128)(2,1)S(1)}, u32[]{:S(2)}, u32[]{:S(2)}) collective-permute-start(bf16[2,108,256]{2,1,0:T(8,128)(2,1)S(1)} %select_bitcast_fusion.9), channel_id=1, source_target_pairs={{0,16},{4,20},{8,24},{12,28},{16,0},{20,4},{24,8},{28,12},{1,17},{... | collective-permute-start | bytes 331784 | tf_op jit(solution)/shard_map/ppermute | solution.py:83
  194.0 8.9 %collective-permute-start.24 = (bf16[2,108,256]{2,1,0:T(8,128)(2,1)S(1)}, bf16[2,108,256]{2,1,0:T(8,128)(2,1)S(1)}, u32[]{:S(2)}, u32[]{:S(2)}) collective-permute-start(bf16[2,108,256]{2,1,0:T(8,128)(2,1)S(1)} %select_bitcast_fusion.8), channel_id=1, source_target_pairs={{0,16},{4,20},{8,24},{12,28},{16,0},{20,4},{24,8},{28,12},{1,17},{... | collective-permute-start | bytes 331784 | tf_op jit(solution)/shard_map/ppermute | solution.py:83
  201.0 4.5 %collective-permute-start.20 = (bf16[108,256]{1,0:T(8,128)(2,1)S(1)}, bf16[108,256]{1,0:T(8,128)(2,1)S(1)}, u32[]{:S(2)}, u32[]{:S(2)}) collective-permute-start(bf16[108,256]{1,0:T(8,128)(2,1)S(1)} %select_bitcast_fusion.12), channel_id=1, source_target_pairs={{0,8},{4,12},{8,0},{12,4},{16,24},{20,28},{24,16},{28,20},{1,9},{5... | collective-permute-start | bytes 165896 | tf_op jit(solution)/shard_map/ppermute | solution.py:83
  202.9 4.9 %collective-permute-start.25 = (bf16[108,256]{1,0:T(8,128)(2,1)S(1)}, bf16[108,256]{1,0:T(8,128)(2,1)S(1)}, u32[]{:S(2)}, u32[]{:S(2)}) collective-permute-start(bf16[108,256]{1,0:T(8,128)(2,1)S(1)} %select_bitcast_fusion.11), channel_id=1, source_target_pairs={{0,8},{4,12},{8,0},{12,4},{16,24},{20,28},{24,16},{28,20},{1,9},{5... | collective-permute-start | bytes 165896 | tf_op jit(solution)/shard_map/ppermute | solution.py:83
  205.8 9.4 %collective-permute-start.29 = (bf16[2,372,128]{2,1,0:T(8,128)(2,1)S(1)}, bf16[2,372,128]{2,1,0:T(8,128)(2,1)S(1)}, u32[]{:S(2)}, u32[]{:S(2)}) collective-permute-start(bf16[2,372,128]{2,1,0:T(8,128)(2,1)S(1)} %select_bitcast_fusion.7), channel_id=1, source_target_pairs={{0,16},{4,20},{8,24},{12,28},{16,0},{20,4},{24,8},{28,12},{1,17},{... | collective-permute-start | bytes 571400 | tf_op jit(solution)/shard_map/ppermute | solution.py:83
  215.3 4.7 %collective-permute-start.30 = (bf16[372,128]{1,0:T(8,128)(2,1)S(1)}, bf16[372,128]{1,0:T(8,128)(2,1)S(1)}, u32[]{:S(2)}, u32[]{:S(2)}) collective-permute-start(bf16[372,128]{1,0:T(8,128)(2,1)S(1)} %select_bitcast_fusion.10), channel_id=1, source_target_pairs={{0,8},{4,12},{8,0},{12,4},{16,24},{20,28},{24,16},{28,20},{1,9},{5... | collective-permute-start | bytes 285704 | tf_op jit(solution)/shard_map/ppermute | solution.py:83
  215.4 17.3 %copy-start.1 = (bf16[384,128]{1,0:T(8,128)(2,1)S(1)}, bf16[384,128]{1,0:T(8,128)(2,1)}, u32[]{:S(2)}) copy-start(bf16[384,128]{1,0:T(8,128)(2,1)} %param.11) | copy-start | bytes 294916
  220.2 7.4 %collective-permute-start.32 = (f32[360,128]{1,0:T(8,128)S(1)}, f32[360,128]{1,0:T(8,128)S(1)}, u32[]{:S(2)}, u32[]{:S(2)}) collective-permute-start(f32[360,128]{1,0:T(8,128)S(1)} %get-tuple-element.127), channel_id=1, source_target_pairs={{1,0},{2,1},{4,2},{6,3},{8,4},{10,5},{11,6},{13,7},{15,8},{17,9},{... | collective-permute-start | bytes 552968 | tf_op jit(solution)/shard_map/ppermute | solution.py:128
  221.5 7.5 %collective-permute-start.31 = (f32[360,128]{1,0:T(8,128)S(1)}, f32[360,128]{1,0:T(8,128)S(1)}, u32[]{:S(2)}, u32[]{:S(2)}) collective-permute-start(f32[360,128]{1,0:T(8,128)S(1)} %get-tuple-element.126), channel_id=1, source_target_pairs={{0,0},{1,1},{3,2},{5,3},{7,4},{9,5},{10,6},{12,7},{14,8},{16,9},{1... | collective-permute-start | bytes 552968 | tf_op jit(solution)/shard_map/ppermute | solution.py:128
  222.2 8.3 %collective-permute-start.33 = (f32[360,128]{1,0:T(8,128)S(1)}, f32[360,128]{1,0:T(8,128)S(1)}, u32[]{:S(2)}, u32[]{:S(2)}) collective-permute-start(f32[360,128]{1,0:T(8,128)S(1)} %get-tuple-element.128), channel_id=1, source_target_pairs={{3,1},{5,2},{7,3},{12,6},{14,7},{16,8},{22,15},{24,16},{25,25},{29... | collective-permute-start | bytes 552968 | tf_op jit(solution)/shard_map/ppermute | solution.py:128
  (7 other events, 11.6 us)

commit v2 on v1

--- a/solution.py
+++ b/solution.py
@@ -1,30 +1,121 @@
+import functools
 import math
 
 import jax
 import jax.numpy as jnp
 import numpy as np
 from jax import lax
+from jax.experimental import pallas as pl
+from jax.experimental.pallas import tpu as pltpu
 from jax.sharding import PartitionSpec as P
 
 dilation_rates = (2, 4, 8)
 both = ("gy", "gz")
-
-
-def extended(cells, sides, width):
-    for axis, dim in sides:
-        count = lax.axis_size(axis)
-        ends = count - 1
-        head = lax.slice_in_dim(cells, 0, width, axis=dim)
-        tail = lax.slice_in_dim(cells, cells.shape[dim] - width, cells.shape[dim], axis=dim)
-        cells = jnp.concatenate(
-            [
-                lax.ppermute(tail, axis, [(i, (i + 1) % count) for i in range(ends)]),
-                cells,
-                lax.ppermute(head, axis, [((i + 1) % count, i) for i in range(ends)]),
-            ],
-            axis=dim,
+directions = ((-1, -1), (-1, 0), (-1, 1), (0, -1), (0, 1), (1, -1), (1, 0), (1, 1))
+send_order = (0, 2, 5, 7, 1, 3, 4, 6)
+
+
+def exchange_kernel(shared, extent, send_ref, out_ref, send_sem, recv_sem):
+    here = (lax.axis_index("gy"), lax.axis_index("gz"))
+    barrier = pltpu.get_barrier_semaphore()
+    places = []
+    for step in directions:
+        place = tuple(at + by for at, by in zip(here, step))
+        inside = None
+        for at, by, size in zip(place, step, extent):
+            if by:
+                test = at >= 0 if by < 0 else at < size
+                inside = test if inside is None else inside & test
+        places.append((place, inside))
+
+    for place, inside in places:
+
+        @pl.when(inside)
+        def _(place=place):
+            pl.semaphore_signal(barrier, inc=1, device_id=place, device_id_type=pl.DeviceIdType.MESH)
+
+    peers = 1
+    for at, size in zip(here, extent):
+        peers = peers * (1 + jnp.where(at > 0, 1, 0) + jnp.where(at < size - 1, 1, 0))
+    pl.semaphore_wait(barrier, peers - 1)
+
+    def copy(way, slot):
+        return pltpu.make_async_remote_copy(
+            src_ref=send_ref.at[0 if shared else way],
+            dst_ref=out_ref.at[slot],
+            send_sem=send_sem.at[way],
+            recv_sem=recv_sem.at[slot],
+            device_id=places[way][0],
+            device_id_type=pl.DeviceIdType.MESH,
         )
-    return cells
+
+    for way in send_order:
+
+        @pl.when(places[way][1])
+        def _(way=way):
+            copy(way, 7 - way).start()
+
+    for way in range(8):
+
+        @pl.when(jnp.logical_not(places[way][1]))
+        def _(way=way):
+            out_ref[way] = jnp.zeros(out_ref.shape[1:], out_ref.dtype)
+
+    for way in range(8):
+
+        @pl.when(places[way][1])
+        def _(way=way):
+            copy(way, way).wait_recv()
+
+    for way in range(8):
+
+        @pl.when(places[way][1])
+        def _(way=way):
+            copy(way, 7 - way).wait_send()
+
+
+def exchange(send, call):
+    extent = (lax.axis_size("gy"), lax.axis_size("gz"))
+    return pl.pallas_call(
+        functools.partial(exchange_kernel, send.shape[0] == 1, extent),
+        out_shape=jax.ShapeDtypeStruct((8, *send.shape[1:]), send.dtype),
+        in_specs=[pl.BlockSpec(memory_space=pltpu.VMEM)],
+        out_specs=pl.BlockSpec(memory_space=pltpu.VMEM),
+        scratch_shapes=[pltpu.SemaphoreType.DMA((8,)), pltpu.SemaphoreType.DMA((8,))],
+        compiler_params=pltpu.CompilerParams(
+            collective_id=call, has_side_effects=True, vmem_limit_bytes=16 * 1024 * 1024
+        ),
+    )(send)
+
+
+def ring_of(cells, width, call):
+    depth, rows, cols, channels = cells.shape
+    if width == 1:
+        send = []
+        for by_y, by_z in directions:
+            piece = cells
+            if by_y:
+                piece = piece[:, :1] if by_y < 0 else piece[:, rows - 1 :]
+            if by_z:
+                piece = piece[:, :, :1] if by_z < 0 else piece[:, :, cols - 1 :]
+            piece = piece.reshape(-1, channels)
+            send.append(jnp.pad(piece, ((0, depth * max(rows, cols) - piece.shape[0]), (0, 0))))
+        got = exchange(jnp.stack(send), call)
+        high, wide = [rows if not by_y else 1 for by_y, _ in directions], [cols if not by_z else 1 for _, by_z in directions]
+        got = [
+            got[way, : depth * high[way] * wide[way]].reshape(depth, high[way], wide[way], channels)
+            for way in range(8)
+        ]
+    else:
+        got = exchange(cells.reshape(1, -1, channels), call)
+        cut_y, cut_z = {-1: slice(rows - width, None), 0: slice(None), 1: slice(0, width)}, {
+            -1: slice(cols - width, None), 0: slice(None), 1: slice(0, width)}
+        got = [
+            got[way].reshape(depth, rows, cols, channels)[:, cut_y[by_y], cut_z[by_z]]
+            for way, (by_y, by_z) in enumerate(directions)
+        ]
+    got.insert(4, cells)
+    return jnp.concatenate([jnp.concatenate(got[at : at + 3], 2) for at in (0, 3, 6)], 1)
 
 
 def silu_slope(value):
@@ -139,7 +230,6 @@
     branch_width = aspp_weight.shape[-1]
     widest_rate = max(dilation_rates)
     count = lax.axis_size("gy") * lax.axis_size("gz")
-    sides = (("gy", 1), ("gz", 2))
     gy_bits, gz_bits = bit_list("gy"), bit_list("gz")
 
     taps = [depth_taps(dilation, depth) for dilation in dilation_rates]
@@ -152,10 +242,10 @@
     )
     block_back = jnp.swapaxes(block_weight.reshape(-1, channels, channels), 1, 2).reshape(-1, channels)
 
-    volume_taps = patches(extended(volume, sides, 1), 1, 1, shape)
+    volume_taps = patches(ring_of(volume, 1, 0), 1, 1, shape)
     pre_block = dot32(volume_taps, block_weight.reshape(-1, channels))
     hidden = jax.nn.silu(pre_block).astype(jnp.bfloat16)
-    hidden_wide = extended(hidden.reshape(*shape, channels), sides, widest_rate)
+    hidden_wide = ring_of(hidden.reshape(*shape, channels), widest_rate, 1)
     hidden_taps = [patches(hidden_wide, widest_rate, dilation, shape) for dilation in dilation_rates]
     branch_pre = jnp.concatenate(
         [
@@ -171,7 +261,7 @@
         grad_rows, proj_weight, (((1,), (1,)), ((), ())), preferred_element_type=jnp.float32
     )
     grad_joined = (proj_back * silu_slope(branch_pre)).astype(jnp.bfloat16)
-    grad_wide = extended(grad_joined.reshape(*shape, -1), sides, widest_rate)
+    grad_wide = ring_of(grad_joined.reshape(*shape, 3 * branch_width), widest_rate, 2)
 
     grad_proj = outer(joined, grad_rows).astype(jnp.bfloat16).reshape(count, -1, branch_width)
     grad_aspp = jnp.concatenate(
@@ -207,7 +297,7 @@
     )
     grad_hidden = dot32(grad_taps, back_weight)
     grad_pre = (grad_hidden * silu_slope(pre_block)).astype(jnp.bfloat16)
-    grad_pre_rim = extended(grad_pre.reshape(*shape, channels), sides, 1)
+    grad_pre_rim = ring_of(grad_pre.reshape(*shape, channels), 1, 3)
 
     grad_block = outer(volume_taps, grad_pre).astype(jnp.bfloat16).reshape(count, -1, channels)
     half = grad_block.shape[1] // 2

time: 236 us -> 238 us (level)
  Pallas kernels: 0 us -> 56.8 us
  waiting for transfers between devices: 91.2 us -> 45.1 us
  starting transfers between devices: 55 us -> 26.1 us
  local copies, waits for them, and re-layouts: 37.5 us -> 47.9 us
  other arithmetic: 26.3 us -> 31.5 us
  matrix products: 14.4 us -> 17.2 us
    pallas_call x0 -> x4, Pallas kernels: none -> 56.8 us  [exchange(): pl.pallas_call(functools.partial(exchange_kernel, send.shape[0] == 1, ext...]
    ppermute x16 -> x0, starting transfers between devices: 38.6 us -> none  [the longest x8 27.8 us: extended(): lax.ppermute(tail, axis, [(i, (i + 1) % count) for i in range(ends)])]
    ppermute x16 -> x0, waiting for transfers between devices: 33.4 us -> none  [the longest x8 25.7 us: extended(): lax.ppermute(head, axis, [((i + 1) % count, i) for i in range(ends)])]
    ppermute x15, waiting for transfers between devices: 53.6 us -> 41 us  [share_of(): lax.ppermute(send, axis, [(i, i ^ 1 << bit) for i in range(sizes[axis])])]
    ppermute x15, starting transfers between devices: 13.8 us -> 23.4 us  [share_of(): lax.ppermute(send, axis, [(i, i ^ 1 << bit) for i in range(sizes[axis])])]
    unnamed x178 -> x245, local copies, waits for them, and re-layouts: 6.94 us -> 14.7 us
    convert_element_type x12, other arithmetic: 2.34 us -> 6.08 us  [share_of(): held = held.astype(jnp.bfloat16)]
    select_n x4, local copies, waits for them, and re-layouts: 3.75 us -> 6.73 us  [share_of(): send = jnp.where(mine == 0, high, low)]
  transfers between devices with their start and end apart: 34 -> 18, of which waited for: 16 -> 11; matrix products, arithmetic and copies ran while one was open for 22% -> 24% of each run, Pallas kernels for 0% -> 15%
where the time goes in v2:
time: 238 us; the launch traced here: 233 us
  Pallas kernels  56.8 us (24%)
  local copies, waits for them, and re-layouts  47.9 us (20%)
  waiting for transfers between devices  45.1 us (19%)
  other arithmetic  31.5 us (13%)
  starting transfers between devices  26.1 us (11%)
  matrix products  17.2 us (7%)
  between operations  8.62 us (4%)
    pallas_call x4, Pallas kernels, exchange(): pl.pallas_call(functools.partial(exchange_kernel, send.shape[0] == 1, ext...  56.8 us
    ppermute x15, waiting for transfers between devices, share_of(): lax.ppermute(send, axis, [(i, i ^ 1 << bit) for i in range(sizes[axis])])  41 us
    ppermute x15, starting transfers between devices, share_of(): lax.ppermute(send, axis, [(i, i ^ 1 << bit) for i in range(sizes[axis])])  23.4 us
    unnamed x245, local copies, waits for them, and re-layouts  14.7 us
    concatenate x9, other arithmetic, ring_of(): jnp.concatenate([jnp.concatenate(got[at:at + 3], 2) for at in (0, 3, 6)], 1)  11.6 us
    dot_general x7, matrix products, dot32(): return jnp.dot(lhs, rhs, preferred_element_type=jnp.float32)  10.5 us
    select_n x4, local copies, waits for them, and re-layouts, share_of(): send = jnp.where(mine == 0, high, low)  6.73 us
    dot_general x5, matrix products, outer(): lax.dot_general(lhs, rhs, (((0,), (0,)), ((), ())), preferred_element_typ...  6.49 us
  transfers between devices with their start and end apart: 18, of which 11 were waited for; matrix products, arithmetic and copies ran while one was open for 24% of the time, Pallas kernels for 15%

profile of v2, /device:TPU:0, one launch (start us, length us, event | category | flops | bytes accessed | tf_op | source)
XLA Modules:
  0.0 233.3 jit_solution(10225116877240685626)
XLA Ops:
  4.2 6.8 %shard_map.119 = bf16[8,32,256]{2,1,0:T(8,128)(2,1)S(1)} custom-call(bf16[8,32,256]{2,1,0:T(8,128)(2,1)S(1)} %constant_dynamic-update-slice_fusion.send_ref), custom_call_target="tpu_custom_call" | custom-call | tf_op jit(solution)/shard_map/pallas_call | solution.py:79
  12.3 1.4 maximum_maximum_fusion.3
  16.3 1.5 copy-done.11
  17.7 1.8 multiply_convert_fusion.1
  19.5 15.3 %shard_map.120 = bf16[8,256,256]{2,1,0:T(8,128)(2,1)S(1)} custom-call(bf16[1,256,256]{2,1,0:T(8,128)(2,1)S(1)} %bitcast.428), custom_call_target="tpu_custom_call" | custom-call | tf_op jit(solution)/shard_map/pallas_call | solution.py:79
  35.3 3.4 %fusion.8 = bf16[8,24,24,256]{3,2,1,0:T(8,128)(2,1)S(1)} fusion(bf16[4,8,8,256]{3,2,1,0:T(8,128)(2,1)S(1)} %bitcast.499, bf16[4,8,8,256]{3,2,1,0:T(8,128)(2,1)S(1)} %bitcast.501, bf16[4,8,8,256]{3,2,1,0:T(8,128)(2,1)S(1)} %bitcast.497, bf16[4,8,8,256]{3,2,1,0:T(8,128)(2,1)S(1)} %bitcast.489, bf16[4,8,8,256]{3,2,1,0:T(8,128)(2,1)S(1)} %bitcast.503, ...), kind=kLoop, calls=%fused_computation.21 | loop fusion | flops 35389440 | bytes 3538944 | tf_op jit(solution)/shard_map/concatenate | solution.py:118
  43.0 2.4 %convolution_convert_fusion.1 = bf16[6912,128]{1,0:T(8,128)(2,1)} fusion(bf16[256,6912]{1,0:T(8,128)(2,1)S(1)} %constant_dynamic-update-slice_fusion.35, bf16[256,384]{1,0:T(8,128)(2,1)S(1)} %fusion.23), kind=kOutput, calls=%fused_computation.1 | convolution fusion | flops 453869568 | bytes 5373952 | tf_op jit(solution)/shard_map/dot_general | solution.py:155
  45.5 1.4 convolution_convert_fusion.3
  46.8 1.3 convolution_convert_fusion.2
  49.2 3.8 %pad_maximum_fusion = bf16[11520,128]{1,0:T(8,128)(2,1)S(1)} fusion(bf16[2304,128]{1,0:T(8,128)(2,1)} %convolution_convert_fusion.2, bf16[2304,128]{1,0:T(8,128)(2,1)} %convolution_convert_fusion.3, bf16[6912,128]{1,0:T(8,128)(2,1)} %convolution_convert_fusion.1), kind=kLoop, calls=%fused_computation.19 | loop fusion | flops 8847360 | bytes 5898240 | tf_op jit(solution)/shard_map/concatenate | solution.py:267
  53.5 2.7 %copy.231 = bf16[2,2,2,2,372,128]{5,3,4,2,1,0:T(2,128)(2,1)} copy(bf16[2,2,2,2,372,128]{5,4,2,1,0,3:T(8,128)(2,1)S(1)} %select_bitcast_fusion) | data formatting | bytes 3047424 | tf_op jit(solution)/shard_map/jit(_where)/select_n | solution.py:173
  56.2 1.9 collective-permute-start.10
  58.1 19.4 %shard_map.121 = bf16[8,256,384]{2,1,0:T(8,128)(2,1)S(1)} custom-call(bf16[1,256,384]{2,1,0:T(8,128)(2,1)S(1)} %bitcast.421), custom_call_target="tpu_custom_call" | custom-call | tf_op jit(solution)/shard_map/pallas_call | solution.py:79
  81.4 2.9 %fusion.18 = bf16[8,24,24,128]{3,2,1,0:T(8,128)(2,1)} fusion(bf16[4,8,8,384]{3,2,1,0:T(8,128)(2,1)S(1)} %bitcast.476, bf16[4,8,8,384]{3,2,1,0:T(8,128)(2,1)S(1)} %bitcast.472, bf16[4,8,8,384]{3,2,1,0:T(8,128)(2,1)S(1)} %bitcast.468, bf16[4,8,8,384]{3,2,1,0:T(8,128)(2,1)S(1)} %bitcast.443, bf16[4,8,8,384]{3,2,1,0:T(8,128)(2,1)S(1)} %bitcast.464, ...), kind=kLoop, calls=%fused_computation.44 | loop fusion | flops 17694720 | bytes 2949120 | tf_op jit(solution)/shard_map/concatenate | solution.py:118
  88.9 2.2 copy.199
  95.7 1.1 convolution_convert_fusion
  97.9 1.6 copy.219
  99.5 5.8 %collective-permute-start = (bf16[2,2,2,2,108,256]{5,3,4,2,1,0:T(2,128)(2,1)}, bf16[2,2,2,2,108,256]{5,3,4,2,1,0:T(2,128)(2,1)}, u32[]{:S(2)}, u32[]{:S(2)}) collective-permute-start(bf16[2,2,2,2,108,256]{5,3,4,2,1,0:T(2,128)(2,1)} %copy.219), channel_id=1, source_target_pairs={{0,4},{4,0},{8,12},{12,8},{16,20},{20,16},{24,28},{28,24},{1,5},{5... | collective-permute-start | bytes 2654216 | tf_op jit(solution)/shard_map/ppermute | solution.py:174
  106.6 1.8 copy.227
  115.7 15.3 %shard_map.122 = bf16[8,32,256]{2,1,0:T(8,128)(2,1)S(1)} custom-call(bf16[8,32,256]{2,1,0:T(8,128)(2,1)S(1)} %constant_dynamic-update-slice_fusion.125.send_ref), custom_call_target="tpu_custom_call" | custom-call | tf_op jit(solution)/shard_map/pallas_call | solution.py:79
  136.5 1.8 copy-done.10
  138.3 5.8 %copy.216 = bf16[27,256,256]{2,1,0:T(8,128)(2,1)} copy(bf16[27,256,256]{1,2,0:T(8,128)(2,1)} %bitcast.484) | data formatting | bytes 7077888 | tf_op jit(solution)/shard_map/transpose | solution.py:243
  144.1 1.3 fusion.57
  147.3 1.4 fusion.58
  148.6 4.9 %convolution_convert_fusion.4 = bf16[4,8,8,256]{3,2,1,0:T(8,128)(2,1)} fusion(bf16[4,8,8,6912]{3,2,1,0:T(8,128)(2,1)} %copy-done.10, bf16[6912,256,1,1]{1,0,3,2:T(8,128)(2,1)} %bitcast.436), kind=kOutput, calls=%fused_computation.56 | convolution fusion | flops 906035200 | bytes 7208960 | tf_op jit(solution)/shard_map/dot_general | solution.py:151
  153.5 1.4 fusion.56
  155.7 1.5 fusion.15
  157.9 1.5 fusion.14
  159.5 1.2 collective-permute-start.6
  160.7 9.6 %collective-permute-done.1 = bf16[2,2,2,108,256]{4,3,2,1,0:T(8,128)(2,1)S(1)} collective-permute-done((bf16[2,2,2,108,256]{4,3,2,1,0:T(8,128)(2,1)S(1)}, bf16[2,2,2,108,256]{4,3,2,1,0:T(8,128)(2,1)S(1)}, u32[]{:S(2)}, u32[]{:S(2)}) %collective-permute-start.1) | collective-permute-done | bytes 442400 | tf_op jit(solution)/shard_map/ppermute | solution.py:174
  170.5 1.7 collective-permute-start.2
  172.7 1.3 collective-permute-start.7
  174.0 1.9 fusion.1
  177.9 3.0 %collective-permute-start.3 = (bf16[2,108,256]{2,1,0:T(8,128)(2,1)S(1)}, bf16[2,108,256]{2,1,0:T(8,128)(2,1)S(1)}, u32[]{:S(2)}, u32[]{:S(2)}) collective-permute-start(bf16[2,108,256]{2,1,0:T(8,128)(2,1)S(1)} %select_bitcast_fusion.9), channel_id=1, source_target_pairs={{0,16},{4,20},{8,24},{12,28},{16,0},{20,4},{24,8},{28,12},{1,17},{... | collective-permute-start | bytes 331784 | tf_op jit(solution)/shard_map/ppermute | solution.py:174
  181.4 3.3 %collective-permute-start.8 = (bf16[2,108,256]{2,1,0:T(8,128)(2,1)S(1)}, bf16[2,108,256]{2,1,0:T(8,128)(2,1)S(1)}, u32[]{:S(2)}, u32[]{:S(2)}) collective-permute-start(bf16[2,108,256]{2,1,0:T(8,128)(2,1)S(1)} %select_bitcast_fusion.8), channel_id=1, source_target_pairs={{0,16},{4,20},{8,24},{12,28},{16,0},{20,4},{24,8},{28,12},{1,17},{... | collective-permute-start | bytes 331784 | tf_op jit(solution)/shard_map/ppermute | solution.py:174
  184.7 4.3 %collective-permute-done.3 = bf16[2,108,256]{2,1,0:T(8,128)(2,1)S(1)} collective-permute-done((bf16[2,108,256]{2,1,0:T(8,128)(2,1)S(1)}, bf16[2,108,256]{2,1,0:T(8,128)(2,1)S(1)}, u32[]{:S(2)}, u32[]{:S(2)}) %collective-permute-start.3) | collective-permute-done | bytes 110624 | tf_op jit(solution)/shard_map/ppermute | solution.py:174
  189.1 1.1 collective-permute-done.8
  190.3 6.0 %collective-permute-done.11 = bf16[2,2,2,372,128]{4,2,3,1,0:T(2,128)(2,1)S(1)} collective-permute-done((bf16[2,2,2,372,128]{4,2,3,1,0:T(2,128)(2,1)S(1)}, bf16[2,2,2,372,128]{4,2,3,1,0:T(2,128)(2,1)S(1)}, u32[]{:S(2)}, u32[]{:S(2)}) %collective-permute-start.11) | collective-permute-done | bytes 761888 | tf_op jit(solution)/shard_map/ppermute | solution.py:174
  196.6 1.3 collective-permute-start.12
  197.9 1.8 collective-permute-start.9
  199.7 6.6 %collective-permute-done.12 = bf16[2,2,372,128]{3,2,1,0:T(8,128)(2,1)S(1)} collective-permute-done((bf16[2,2,372,128]{3,2,1,0:T(8,128)(2,1)S(1)}, bf16[2,2,372,128]{3,2,1,0:T(8,128)(2,1)S(1)}, u32[]{:S(2)}, u32[]{:S(2)}) %collective-permute-start.12) | collective-permute-done | bytes 380960 | tf_op jit(solution)/shard_map/ppermute | solution.py:174
  207.2 8.6 %collective-permute-done.13 = bf16[2,372,128]{2,1,0:T(8,128)(2,1)S(1)} collective-permute-done((bf16[2,372,128]{2,1,0:T(8,128)(2,1)S(1)}, bf16[2,372,128]{2,1,0:T(8,128)(2,1)S(1)}, u32[]{:S(2)}, u32[]{:S(2)}) %collective-permute-start.13) | collective-permute-done | bytes 190496 | tf_op jit(solution)/shard_map/ppermute | solution.py:174
  216.8 3.8 %collective-permute-done.14 = bf16[372,128]{1,0:T(8,128)(2,1)S(1)} collective-permute-done((bf16[372,128]{1,0:T(8,128)(2,1)S(1)}, bf16[372,128]{1,0:T(8,128)(2,1)S(1)}, u32[]{:S(2)}, u32[]{:S(2)}) %collective-permute-start.14) | collective-permute-done | bytes 95264 | tf_op jit(solution)/shard_map/ppermute | solution.py:174
  220.8 1.3 collective-permute-start.16
  224.1 4.2 %collective-permute-done.16 = f32[360,128]{1,0:T(8,128)S(1)} collective-permute-done((f32[360,128]{1,0:T(8,128)S(1)}, f32[360,128]{1,0:T(8,128)S(1)}, u32[]{:S(2)}, u32[]{:S(2)}) %collective-permute-start.16) | collective-permute-done | bytes 184352 | tf_op jit(solution)/shard_map/ppermute | solution.py:219
  228.3 1.3 dynamic_update_slice.10
  229.6 1.4 dynamic_update_slice.9
  231.1 1.4 dynamic_update_slice.11
  (374 shorter events, 46.5 us)
Async XLA Ops:
  0.6 42.2 %copy-start = (bf16[384,128]{1,0:T(8,128)(2,1)S(1)}, bf16[384,128]{1,0:T(8,128)(2,1)}, u32[]{:S(2)}) copy-start(bf16[384,128]{1,0:T(8,128)(2,1)} %param.11) | copy-start | bytes 294916
  15.3 2.4 %copy-start.11 = (bf16[3,3,3,256,256]{4,3,2,1,0:T(8,128)(2,1)S(1)}, bf16[3,3,3,256,256]{4,3,2,1,0:T(8,128)(2,1)}, u32[]{:S(2)}) copy-start(bf16[3,3,3,256,256]{4,3,2,1,0:T(8,128)(2,1)} %param.9) | copy-start | bytes 10616836
  16.3 3.3 %copy-start.7 = (bf16[256,6912]{1,0:T(8,128)(2,1)}, bf16[256,6912]{1,0:T(8,128)(2,1)S(1)}, u32[]{:S(2)}) copy-start(bf16[256,6912]{1,0:T(8,128)(2,1)S(1)} %constant_dynamic-update-slice_fusion.8) | copy-start | bytes 10616836
  17.7 21.0 %slice-start = ((s8[5308416]{0:T(1024)(128)(4,1)}), s8[4194304]{0:T(1024)(128)(4,1)S(1)}, s32[]{:S(2)}) async-start(s8[5308416]{0:T(1024)(128)(4,1)} %bitcast.494), calls=%async_computation | async-start | bytes 8388608
  19.5 19.2 %slice-start.1 = ((s8[5308416]{0:T(1024)(128)(4,1)}), s8[1114112]{0:T(1024)(128)(4,1)S(1)}, s32[]{:S(2)}) async-start(s8[5308416]{0:T(1024)(128)(4,1)} %bitcast.494), calls=%async_computation.1 | async-start | bytes 2228224
  53.3 2.9 %copy-start.1 = (bf16[2,2,1,2,2,372,128]{6,5,4,3,2,1,0:T(8,128)(2,1)}, bf16[2,2,1,2,2,372,128]{6,5,4,3,2,1,0:T(8,128)(2,1)S(1)}, u32[]{:S(2)}) copy-start(bf16[2,2,1,2,2,372,128]{6,5,4,3,2,1,0:T(8,128)(2,1)S(1)} %get-tuple-element.9) | copy-start | bytes 4571140
  53.3 2.9 %copy-start.3 = (bf16[2,2,1,2,2,372,128]{6,5,4,3,2,1,0:T(8,128)(2,1)}, bf16[2,2,1,2,2,372,128]{6,5,4,3,2,1,0:T(8,128)(2,1)S(1)}, u32[]{:S(2)}) copy-start(bf16[2,2,1,2,2,372,128]{6,5,4,3,2,1,0:T(8,128)(2,1)S(1)} %get-tuple-element.10) | copy-start | bytes 4571140
  56.2 117.8 %collective-permute-start.10 = (bf16[2,2,2,2,372,128]{5,3,4,2,1,0:T(2,128)(2,1)}, bf16[2,2,2,2,372,128]{5,3,4,2,1,0:T(2,128)(2,1)}, u32[]{:S(2)}, u32[]{:S(2)}) collective-permute-start(bf16[2,2,2,2,372,128]{5,3,4,2,1,0:T(2,128)(2,1)} %copy.231), channel_id=1, source_target_pairs={{0,4},{4,0},{8,12},{12,8},{16,20},{20,16},{24,28},{28,24},{1,5},{5... | collective-permute-start | bytes 4571144 | tf_op jit(solution)/shard_map/ppermute | solution.py:174
  88.9 2.2 copy-start.9
  91.2 1.3 copy-start.28
  91.2 1.3 copy-start.27
  91.2 1.4 copy-start.26
  91.3 1.4 copy-start.25
  91.3 1.4 copy-start.24
  91.3 1.4 copy-start.23
  91.3 1.5 copy-start.22
  91.3 1.5 copy-start.21
  91.6 1.3 copy-start.19
  91.7 1.4 copy-start.20
  91.7 1.4 copy-start.38
  91.7 1.6 copy-start.13
  91.7 1.7 copy-start.17
  91.7 1.9 copy-start.18
  91.7 2.0 copy-start.43
  93.7 2.0 copy-start.8
  99.5 56.2 %collective-permute-start = (bf16[2,2,2,2,108,256]{5,3,4,2,1,0:T(2,128)(2,1)}, bf16[2,2,2,2,108,256]{5,3,4,2,1,0:T(2,128)(2,1)}, u32[]{:S(2)}, u32[]{:S(2)}) collective-permute-start(bf16[2,2,2,2,108,256]{5,3,4,2,1,0:T(2,128)(2,1)} %copy.219), channel_id=1, source_target_pairs={{0,4},{4,0},{8,12},{12,8},{16,20},{20,16},{24,28},{28,24},{1,5},{5... | collective-permute-start | bytes 2654216 | tf_op jit(solution)/shard_map/ppermute | solution.py:174
  108.4 49.5 %collective-permute-start.5 = (bf16[2,2,2,2,108,256]{5,3,4,2,1,0:T(2,128)(2,1)}, bf16[2,2,2,2,108,256]{5,3,4,2,1,0:T(2,128)(2,1)}, u32[]{:S(2)}, u32[]{:S(2)}) collective-permute-start(bf16[2,2,2,2,108,256]{5,3,4,2,1,0:T(2,128)(2,1)} %copy.227), channel_id=1, source_target_pairs={{0,4},{4,0},{8,12},{12,8},{16,20},{20,16},{24,28},{28,24},{1,5},{5... | collective-permute-start | bytes 2654216 | tf_op jit(solution)/shard_map/ppermute | solution.py:174
  132.6 3.5 %copy-start.16 = (bf16[4,9,10,256]{3,2,1,0:T(8,128)(2,1)S(1)}, bf16[4,9,10,256]{3,2,1,0:T(8,128)(2,1)}, u32[]{:S(2)}) copy-start(bf16[4,9,10,256]{3,2,1,0:T(8,128)(2,1)} %get-tuple-element.123) | copy-start | bytes 552964
  136.5 1.8 copy-start.10
  148.6 6.2 %copy-start.15 = (bf16[256,384]{1,0:T(8,128)(2,1)S(1)}, bf16[256,384]{1,0:T(8,128)(2,1)}, u32[]{:S(2)}) copy-start(bf16[256,384]{1,0:T(8,128)(2,1)} %copy-done.14) | copy-start | bytes 589828
  153.5 4.4 %copy-start.6 = (bf16[2,2,1,2,2,108,256]{6,5,4,3,2,1,0:T(8,128)(2,1)S(1)}, bf16[2,2,1,2,2,108,256]{6,5,4,3,2,1,0:T(8,128)(2,1)}, u32[]{:S(2)}) copy-start(bf16[2,2,1,2,2,108,256]{6,5,4,3,2,1,0:T(8,128)(2,1)} %copy-done.5) | copy-start | bytes 2654212
  157.2 13.0 %collective-permute-start.1 = (bf16[2,2,2,108,256]{4,3,2,1,0:T(8,128)(2,1)S(1)}, bf16[2,2,2,108,256]{4,3,2,1,0:T(8,128)(2,1)S(1)}, u32[]{:S(2)}, u32[]{:S(2)}) collective-permute-start(bf16[2,2,2,108,256]{4,3,2,1,0:T(8,128)(2,1)S(1)} %select_bitcast_fusion.5), channel_id=1, source_target_pairs={{0,1},{1,0},{2,3},{3,2},{4,5},{5,4},{6,7},{7,6},{8,9},{9,8},{10,11... | collective-permute-start | bytes 1327112 | tf_op jit(solution)/shard_map/ppermute | solution.py:174
  159.4 14.6 %copy-start.2 = (bf16[2,2,1,2,2,372,128]{6,5,4,3,2,1,0:T(8,128)(2,1)S(1)}, bf16[2,2,1,2,2,372,128]{6,5,4,3,2,1,0:T(8,128)(2,1)}, u32[]{:S(2)}) copy-start(bf16[2,2,1,2,2,372,128]{6,5,4,3,2,1,0:T(8,128)(2,1)} %copy-done.1) | copy-start | bytes 4571140
  159.4 14.6 %copy-start.4 = (bf16[2,2,1,2,2,372,128]{6,5,4,3,2,1,0:T(8,128)(2,1)S(1)}, bf16[2,2,1,2,2,372,128]{6,5,4,3,2,1,0:T(8,128)(2,1)}, u32[]{:S(2)}) copy-start(bf16[2,2,1,2,2,372,128]{6,5,4,3,2,1,0:T(8,128)(2,1)} %copy-done.3) | copy-start | bytes 4571140
  159.5 13.0 %collective-permute-start.6 = (bf16[2,2,2,108,256]{4,3,1,0,2:T(8,128)(2,1)S(1)}, bf16[2,2,2,108,256]{4,3,1,0,2:T(8,128)(2,1)S(1)}, u32[]{:S(2)}, u32[]{:S(2)}) collective-permute-start(bf16[2,2,2,108,256]{4,3,1,0,2:T(8,128)(2,1)S(1)} %select_bitcast_fusion.4), channel_id=1, source_target_pairs={{0,2},{1,3},{2,0},{3,1},{4,6},{5,7},{6,4},{7,5},{8,10},{9,11},{10,... | collective-permute-start | bytes 1327112 | tf_op jit(solution)/shard_map/ppermute | solution.py:174
  170.5 7.3 %collective-permute-start.2 = (bf16[2,2,108,256]{3,2,1,0:T(8,128)(2,1)S(1)}, bf16[2,2,108,256]{3,2,1,0:T(8,128)(2,1)S(1)}, u32[]{:S(2)}, u32[]{:S(2)}) collective-permute-start(bf16[2,2,108,256]{3,2,1,0:T(8,128)(2,1)S(1)} %fusion.45), channel_id=1, source_target_pairs={{0,2},{1,3},{2,0},{3,1},{4,6},{5,7},{6,4},{7,5},{8,10},{9,11},{10,... | collective-permute-start | bytes 663560 | tf_op jit(solution)/shard_map/ppermute | solution.py:174
  172.7 8.6 %collective-permute-start.7 = (bf16[2,2,108,256]{3,2,1,0:T(8,128)(2,1)S(1)}, bf16[2,2,108,256]{3,2,1,0:T(8,128)(2,1)S(1)}, u32[]{:S(2)}, u32[]{:S(2)}) collective-permute-start(bf16[2,2,108,256]{3,2,1,0:T(8,128)(2,1)S(1)} %select_bitcast_fusion.6), channel_id=1, source_target_pairs={{0,1},{1,0},{2,3},{3,2},{4,5},{5,4},{6,7},{7,6},{8,9},{9,8},{10,11... | collective-permute-start | bytes 663560 | tf_op jit(solution)/shard_map/ppermute | solution.py:174
  176.6 19.7 %collective-permute-start.11 = (bf16[2,2,2,372,128]{4,2,3,1,0:T(2,128)(2,1)S(1)}, bf16[2,2,2,372,128]{4,2,3,1,0:T(2,128)(2,1)S(1)}, u32[]{:S(2)}, u32[]{:S(2)}) collective-permute-start(bf16[2,2,2,372,128]{4,2,3,1,0:T(2,128)(2,1)S(1)} %copy.233), channel_id=1, source_target_pairs={{0,1},{1,0},{2,3},{3,2},{4,5},{5,4},{6,7},{7,6},{8,9},{9,8},{10,11... | collective-permute-start | bytes 2285576 | tf_op jit(solution)/shard_map/ppermute | solution.py:174
  177.9 11.1 %collective-permute-start.3 = (bf16[2,108,256]{2,1,0:T(8,128)(2,1)S(1)}, bf16[2,108,256]{2,1,0:T(8,128)(2,1)S(1)}, u32[]{:S(2)}, u32[]{:S(2)}) collective-permute-start(bf16[2,108,256]{2,1,0:T(8,128)(2,1)S(1)} %select_bitcast_fusion.9), channel_id=1, source_target_pairs={{0,16},{4,20},{8,24},{12,28},{16,0},{20,4},{24,8},{28,12},{1,17},{... | collective-permute-start | bytes 331784 | tf_op jit(solution)/shard_map/ppermute | solution.py:174
  181.4 8.9 %collective-permute-start.8 = (bf16[2,108,256]{2,1,0:T(8,128)(2,1)S(1)}, bf16[2,108,256]{2,1,0:T(8,128)(2,1)S(1)}, u32[]{:S(2)}, u32[]{:S(2)}) collective-permute-start(bf16[2,108,256]{2,1,0:T(8,128)(2,1)S(1)} %select_bitcast_fusion.8), channel_id=1, source_target_pairs={{0,16},{4,20},{8,24},{12,28},{16,0},{20,4},{24,8},{28,12},{1,17},{... | collective-permute-start | bytes 331784 | tf_op jit(solution)/shard_map/ppermute | solution.py:174
  189.1 10.7 %collective-permute-start.4 = (bf16[108,256]{1,0:T(8,128)(2,1)S(1)}, bf16[108,256]{1,0:T(8,128)(2,1)S(1)}, u32[]{:S(2)}, u32[]{:S(2)}) collective-permute-start(bf16[108,256]{1,0:T(8,128)(2,1)S(1)} %select_bitcast_fusion.12), channel_id=1, source_target_pairs={{0,8},{4,12},{8,0},{12,4},{16,24},{20,28},{24,16},{28,20},{1,9},{5... | collective-permute-start | bytes 165896 | tf_op jit(solution)/shard_map/ppermute | solution.py:174
  196.6 9.7 %collective-permute-start.12 = (bf16[2,2,372,128]{3,2,1,0:T(8,128)(2,1)S(1)}, bf16[2,2,372,128]{3,2,1,0:T(8,128)(2,1)S(1)}, u32[]{:S(2)}, u32[]{:S(2)}) collective-permute-start(bf16[2,2,372,128]{3,2,1,0:T(8,128)(2,1)S(1)} %fusion.41), channel_id=1, source_target_pairs={{0,2},{1,3},{2,0},{3,1},{4,6},{5,7},{6,4},{7,5},{8,10},{9,11},{10,... | collective-permute-start | bytes 1142792 | tf_op jit(solution)/shard_map/ppermute | solution.py:174
  197.9 9.3 %collective-permute-start.9 = (bf16[108,256]{1,0:T(8,128)(2,1)S(1)}, bf16[108,256]{1,0:T(8,128)(2,1)S(1)}, u32[]{:S(2)}, u32[]{:S(2)}) collective-permute-start(bf16[108,256]{1,0:T(8,128)(2,1)S(1)} %select_bitcast_fusion.11), channel_id=1, source_target_pairs={{0,8},{4,12},{8,0},{12,4},{16,24},{20,28},{24,16},{28,20},{1,9},{5... | collective-permute-start | bytes 165896 | tf_op jit(solution)/shard_map/ppermute | solution.py:174
  206.6 9.2 %collective-permute-start.13 = (bf16[2,372,128]{2,1,0:T(8,128)(2,1)S(1)}, bf16[2,372,128]{2,1,0:T(8,128)(2,1)S(1)}, u32[]{:S(2)}, u32[]{:S(2)}) collective-permute-start(bf16[2,372,128]{2,1,0:T(8,128)(2,1)S(1)} %select_bitcast_fusion.7), channel_id=1, source_target_pairs={{0,16},{4,20},{8,24},{12,28},{16,0},{20,4},{24,8},{28,12},{1,17},{... | collective-permute-start | bytes 571400 | tf_op jit(solution)/shard_map/ppermute | solution.py:174
  215.9 4.7 %collective-permute-start.14 = (bf16[372,128]{1,0:T(8,128)(2,1)S(1)}, bf16[372,128]{1,0:T(8,128)(2,1)S(1)}, u32[]{:S(2)}, u32[]{:S(2)}) collective-permute-start(bf16[372,128]{1,0:T(8,128)(2,1)S(1)} %select_bitcast_fusion.10), channel_id=1, source_target_pairs={{0,8},{4,12},{8,0},{12,4},{16,24},{20,28},{24,16},{28,20},{1,9},{5... | collective-permute-start | bytes 285704 | tf_op jit(solution)/shard_map/ppermute | solution.py:174
  220.8 7.4 %collective-permute-start.16 = (f32[360,128]{1,0:T(8,128)S(1)}, f32[360,128]{1,0:T(8,128)S(1)}, u32[]{:S(2)}, u32[]{:S(2)}) collective-permute-start(f32[360,128]{1,0:T(8,128)S(1)} %get-tuple-element.137), channel_id=1, source_target_pairs={{1,0},{2,1},{4,2},{6,3},{8,4},{10,5},{11,6},{13,7},{15,8},{17,9},{... | collective-permute-start | bytes 552968 | tf_op jit(solution)/shard_map/ppermute | solution.py:219
  222.1 7.5 %collective-permute-start.15 = (f32[360,128]{1,0:T(8,128)S(1)}, f32[360,128]{1,0:T(8,128)S(1)}, u32[]{:S(2)}, u32[]{:S(2)}) collective-permute-start(f32[360,128]{1,0:T(8,128)S(1)} %get-tuple-element.136), channel_id=1, source_target_pairs={{0,0},{1,1},{3,2},{5,3},{7,4},{9,5},{10,6},{12,7},{14,8},{16,9},{1... | collective-permute-start | bytes 552968 | tf_op jit(solution)/shard_map/ppermute | solution.py:219
  222.8 8.3 %collective-permute-start.17 = (f32[360,128]{1,0:T(8,128)S(1)}, f32[360,128]{1,0:T(8,128)S(1)}, u32[]{:S(2)}, u32[]{:S(2)}) collective-permute-start(f32[360,128]{1,0:T(8,128)S(1)} %get-tuple-element.138), channel_id=1, source_target_pairs={{3,1},{5,2},{7,3},{12,6},{14,7},{16,8},{22,15},{24,16},{25,25},{29... | collective-permute-start | bytes 552968 | tf_op jit(solution)/shard_map/ppermute | solution.py:219
  (16 other events, 15.9 us)
